TPU v7x, 512 devices: a whole 4x8x8 slice. The times are simulated.
512 devices in a mesh: blk: 8 (over y), uly: 8 (over x, core), tp: 8 (over z).
Axes of the slice: x: 4, y: 8, z: 8, core: 2. Of those that a mesh axis runs over, the one named last changes fastest.
Arguments:
- queries: bfloat16 [8192, 64, 128], P(('blk', 'uly'), 'tp'), may hold values from -84 to 84
- keys: bfloat16 [8192, 8, 128], P(('blk', 'uly'), 'tp'), may hold values from -12 to 12
- values: bfloat16 [8192, 8, 128], P(('blk', 'uly'), 'tp'), may hold values from -6 to 6
- span_order: int32 [16], replicated, may hold values from 0 to 15, each once
Outputs:
- attended: bfloat16 [8192, 64, 128], P(('blk', 'uly'), 'tp')
Inputs may be any that keep to these rules, and one draw needn't show every extreme that they name: `span_order`: holds every number from 0 to 15 exactly once.
All inputs are finite; a program needn't handle non-finite values.
Results may differ from a plain program's by a relative error of at most 0.0065.
Values may be sent and summed in bfloat16 or wider, within the bound.
No kernel may reach another device: no remote copies, remote signals or barrier semaphores. Data moves between devices by JAX's collectives and lax.ppermute only.
A program may use at most 64 MiB of HBM per device.

v0:
```python
import math

import jax
import jax.numpy as jnp
from jax import lax
from jax.sharding import PartitionSpec as P


def span_positions(row_index, span_order, span_len):
    span_index = row_index // span_len
    span_ids = jnp.arange(span_order.shape[0], dtype=jnp.int32)
    span_hit = span_index[:, None] == span_ids[None, :]
    start_pos = jnp.sum(jnp.where(span_hit, span_order[None, :], 0), axis=1)
    return start_pos * span_len + row_index % span_len


def attend_block(carry_state, query_four, query_pos, key_block, value_block, key_pos, score_scale):
    running_max, running_sum, weighted = carry_state
    scores = (
        jnp.einsum("rhgd,phd->rhgp", query_four, key_block, preferred_element_type=jnp.float32)
        * score_scale
    )
    visible = (key_pos[None, :] <= query_pos[:, None])[:, None, None, :]
    scores = jnp.where(visible, scores, -1e30)
    next_max = jnp.maximum(running_max, jnp.max(scores, axis=3))
    weights = jnp.where(visible, jnp.exp(scores - next_max[..., None]), 0.0)
    rescale = jnp.exp(running_max - next_max)
    running_sum = running_sum * rescale + jnp.sum(weights, axis=3)
    weighted = weighted * rescale[..., None] + jnp.einsum(
        "rhgp,phd->rhgd",
        weights.astype(jnp.bfloat16),
        value_block,
        preferred_element_type=jnp.float32,
    )
    return (next_max, running_sum, weighted)


def make_folder(query_four, query_pos, span_order, span_len):
    score_scale = 1.0 / math.sqrt(query_four.shape[3])

    def fold_keys(carry_state, key_piece, start):
        piece_keys, piece_values = key_piece
        piece_rows = piece_keys.shape[0]
        block_rows = 512
        block_count = piece_rows // block_rows
        heads_here = piece_keys.shape[1]
        head_size = piece_keys.shape[2]
        key_blocks = piece_keys.reshape(block_count, block_rows, heads_here, head_size)
        value_blocks = piece_values.reshape(block_count, block_rows, heads_here, head_size)
        key_positions = span_positions(
            jnp.arange(piece_rows, dtype=jnp.int32), span_order, span_len
        )
        key_positions = key_positions.reshape(block_count, block_rows)

        def scan_step(inner_state, block_item):
            key_block, value_block, key_pos = block_item
            inner_state = attend_block(
                inner_state, query_four, query_pos, key_block, value_block, key_pos, score_scale
            )
            return (inner_state, None)

        carry_state, _ = lax.scan(scan_step, carry_state, (key_blocks, value_blocks, key_positions))
        return carry_state

    return fold_keys


def initial_state(query_four):
    lead_shape = query_four.shape[:3]
    return (
        jnp.full(lead_shape, -1e30, jnp.float32),
        jnp.zeros(lead_shape, jnp.float32),
        jnp.zeros(query_four.shape, jnp.float32),
    )


def finish_state(final_state):
    running_max, running_sum, weighted = final_state
    return (weighted / running_sum[..., None]).astype(jnp.bfloat16)


def local(queries, keys, values, span_order):
    tok_rows = queries.shape[0]
    head_size = queries.shape[2]
    uly_size = lax.axis_size("uly")
    span_len = tok_rows * uly_size // 2
    blk_place = lax.axis_index("blk")
    query_heads = lax.all_to_all(queries, "uly", split_axis=1, concat_axis=0, tiled=True)
    local_rows = query_heads.shape[0]
    per_device = query_heads.shape[1]
    query_four = query_heads.reshape(local_rows, 1, per_device, head_size)
    query_pos = span_positions(
        blk_place * local_rows + jnp.arange(local_rows, dtype=jnp.int32), span_order, span_len
    )
    folder = make_folder(query_four, query_pos, span_order, span_len)
    final_state = folder(
        initial_state(query_four),
        (
            lax.all_gather(keys, ("blk", "uly"), axis=0, tiled=True),
            lax.all_gather(values, ("blk", "uly"), axis=0, tiled=True),
        ),
        jnp.int32(0),
    )
    head_output = finish_state(final_state).reshape(local_rows, per_device, head_size)
    return lax.all_to_all(head_output, "uly", split_axis=0, concat_axis=1, tiled=True)


def solution(mesh):
    in_specs = (
        P(("blk", "uly"), "tp", None),
        P(("blk", "uly"), "tp", None),
        P(("blk", "uly"), "tp", None),
        P(),
    )
    out_specs = P(("blk", "uly"), "tp", None)
    return jax.shard_map(local, mesh=mesh, in_specs=in_specs, out_specs=out_specs, check_vma=False)
```

profile of v0, /device:TPU:1, one launch (start us, length us, event | category | flops | bytes accessed | tf_op | source)
XLA Modules:
  0.0 263.5 jit_solution(8121300190383267117)
XLA Ops:
  8.0 1.7 copy.22
  9.7 10.2 %all-to-all-start = ((bf16[128,8,128]{2,0,1:T(8,128)(2,1)}), bf16[128,8,128]{2,0,1:T(8,128)(2,1)S(1)}, u32[]{:S(2)}, u32[]{:S(2)}) async-start(bf16[128,8,128]{2,0,1:T(8,128)(2,1)} %copy.22), calls=%async_computation | async-start | bytes 524288 | tf_op jit(solution)/shard_map/all_to_all | solution.py:88
  21.6 4.8 %all-to-all-done = bf16[128,8,128]{2,0,1:T(8,128)(2,1)S(1)} async-done(((bf16[128,8,128]{2,0,1:T(8,128)(2,1)}), bf16[128,8,128]{2,0,1:T(8,128)(2,1)S(1)}, u32[]{:S(2)}, u32[]{:S(2)}) %all-to-all-start) | async-done | bytes 262176 | tf_op jit(solution)/shard_map/all_to_all | solution.py:88
  26.4 72.7 %all-gather.3.cloned.1.call-done = bf16[8192,1,128]{2,0,1:T(8,128)(2,1)} async-done(((bf16[128,1,128]{2,0,1:T(8,128)(2,1)}), bf16[8192,1,128]{2,0,1:T(8,128)(2,1)}) %all-gather.3.cloned.1.call-update) | async-done | bytes 2097168 | tf_op jit(solution)/shard_map/all_gather | solution.py:99
  99.1 83.9 %all-gather.5.cloned.1.call-done = bf16[8192,1,128]{2,0,1:T(8,128)(2,1)} async-done(((bf16[128,1,128]{2,0,1:T(8,128)(2,1)}), bf16[8192,1,128]{2,0,1:T(8,128)(2,1)}) %all-gather.5.cloned.1.call-update) | async-done | bytes 2097168 | tf_op jit(solution)/shard_map/all_gather | solution.py:100
  183.0 60.9 %while.15 = (s32[]{:T(128)}, f32[1024,1,1]{0,2,1:T(1,128)S(1)}, f32[1024,1,1]{0,2,1:T(1,128)S(1)}, f32[1024,1,1,128]{0,3,2,1:T(8,128)S(1)}, s32[16,512]{1,0:T(8,...) while((s32[]{:T(128)}, f32[1024,1,1]{0,2,1:T(1,128)S(1)}, ...), condition=%wide.region_5.6_spmd.clone, body=%wide.region_2.5_spmd.clone.sunk | while | flops 277222400 | bytes 7953533 | solution.py:62
  185.0 1.7 fusion.51
  188.8 1.7 fusion.51
  190.6 1.4 fusion.47
  192.7 1.7 fusion.51
  196.5 1.7 fusion.51
  200.3 1.7 fusion.51
  204.1 1.7 fusion.51
  207.9 1.7 fusion.51
  211.7 1.7 fusion.51
  215.5 1.7 fusion.51
  219.3 1.7 fusion.51
  223.1 1.7 fusion.51
  226.9 1.7 fusion.51
  230.7 1.7 fusion.51
  234.5 1.7 fusion.51
  238.3 1.7 fusion.51
  242.1 1.7 fusion.51
  245.7 9.8 %all_to_all.33 = bf16[8,2,8192]{2,1,0:T(2,128)(2,1)S(1)} all-to-all(bf16[8,2,8192]{2,1,0:T(2,128)(2,1)S(1)} %reshape.133), channel_id=1, replica_groups=mesh['blk'=8,'uly'=8,'tp'=8] {'uly'}, dimensions={0} | all-to-all | bytes 524288 | tf_op jit(solution)/shard_map/all_to_all | solution.py:105
  (118 shorter events, 37.4 us)
Async XLA Ops:
  6.5 92.5 %all-gather.3.cloned.1.call-start = ((), (), s32[]{:S(2)}) async-start(), calls=%async_computation.2 | async-start | bytes 2129920 | tf_op jit(solution)/shard_map/all_gather | solution.py:99
  7.3 175.7 %all-gather.5.cloned.1.call-start = ((), (), s32[]{:S(2)}) async-start(), calls=%async_computation.3 | async-start | bytes 2129920 | tf_op jit(solution)/shard_map/all_gather | solution.py:100
  9.7 16.7 %all-to-all-start = ((bf16[128,8,128]{2,0,1:T(8,128)(2,1)}), bf16[128,8,128]{2,0,1:T(8,128)(2,1)S(1)}, u32[]{:S(2)}, u32[]{:S(2)}) async-start(bf16[128,8,128]{2,0,1:T(8,128)(2,1)} %copy.22), calls=%async_computation | async-start | bytes 524288 | tf_op jit(solution)/shard_map/all_to_all | solution.py:88
Sparse Core Ops, SparseCore 0:
  10.7 88.3 all-gather.2
  102.4 80.5 all-gather.4
where the time goes:
time: 264 us; the launch traced here: 263 us
  waiting for transfers between devices  163 us (62%)
  matrix products  49 us (19%)
  between operations  13.5 us (5%)
  other arithmetic  13.2 us (5%)
  starting transfers between devices  10.2 us (4%)
  blocking collectives  9.79 us (4%)
  local copies, waits for them, and re-layouts  3.84 us (1%)
    all_gather x1, waiting for transfers between devices, local(): lax.all_gather(values, ('blk', 'uly'), axis=0, tiled=True)  83.9 us
    all_gather x1, waiting for transfers between devices, local(): lax.all_gather(keys, ('blk', 'uly'), axis=0, tiled=True)  72.7 us
    dot_general x16, matrix products, attend_block(): jnp.einsum('rhgp,phd->rhgd', weights.astype(jnp.bfloat16), value_block, p...  27.1 us
    dot_general x16, matrix products, attend_block(): jnp.einsum('rhgd,phd->rhgp', query_four, key_block, preferred_element_typ...  21.9 us
    all_to_all x1, starting transfers between devices, local(): lax.all_to_all(queries, 'uly', split_axis=1, concat_axis=0, tiled=True)  10.2 us
    reduce_sum x16, other arithmetic, attend_block(): running_sum = running_sum * rescale + jnp.sum(weights, axis=3)  9.98 us
    all_to_all x1, blocking collectives, local(): lax.all_to_all(head_output, 'uly', split_axis=0, concat_axis=1, tiled=True)  9.79 us
  transfers between devices with their start and end apart: 3, of which 3 were waited for; matrix products, arithmetic and copies ran while one was open for 1% of the time, Pallas kernels for 0%

commit v1 on v0

v1 whole, which is shorter than its diff:
```python
import math

import jax
import jax.numpy as jnp
from jax import lax
from jax.experimental import pallas as pl
from jax.experimental.pallas import tpu as pltpu
from jax.sharding import Mesh, PartitionSpec as P

LOG2E = 1.4426950408889634
MASKED = -1.5e38
START = -1.0e30
ROW_BLOCK = 256


def attend_kernel(first, last, peers, rows, heads, info, q_ref, kv_ref, *refs):
    if not first:
        m_in, l_in, a_in, *refs = refs
    if last:
        out_ref, m_ref, l_ref, a_ref = refs
    else:
        m_ref, l_ref, a_ref = refs
    if first:
        m_ref[...] = jnp.full(m_ref.shape, START, jnp.float32)
        l_ref[...] = jnp.zeros(l_ref.shape, jnp.float32)
        a_ref[...] = jnp.zeros(a_ref.shape, jnp.float32)
    else:
        m_ref[...] = m_in[...]
        l_ref[...] = l_in[...]
        a_ref[...] = a_in[...]
    total_rows, head_size = q_ref.shape
    spans = 16
    per_span = peers // spans
    keys = per_span * rows
    own_span = info[spans]
    query_start = info[spans + 1]
    key_start = info[spans + 2]
    factor = LOG2E / math.sqrt(head_size)

    def fold(j, diagonal):
        block = kv_ref[pl.ds(j * per_span, per_span)]
        k = block[:, :rows].reshape(keys, head_size)
        v = block[:, rows:].reshape(keys, head_size)
        for r in range(0, total_rows, ROW_BLOCK):
            at = pl.ds(r, ROW_BLOCK)
            s = lax.dot_general(
                q_ref[at, :], k, (((1,), (1,)), ((), ())), preferred_element_type=jnp.float32
            ) * factor
            if diagonal:
                row = lax.broadcasted_iota(jnp.int32, s.shape, 0) + r
                col = lax.broadcasted_iota(jnp.int32, s.shape, 1)
                q_off = query_start + row // heads
                k_off = key_start + (col // rows) * (2 * rows) + col % rows
                s = jnp.where(k_off <= q_off, s, MASKED)
            m_old = m_ref[at, :]
            m_new = jnp.maximum(m_old, jnp.max(s, axis=1, keepdims=True))
            alpha = jnp.exp2(m_old - m_new)
            p = jnp.exp2(s - jnp.tile(m_new, (1, keys // 128)))
            part = p[:, :128]
            for c in range(128, keys, 128):
                part = part + p[:, c : c + 128]
            m_ref[at, :] = m_new
            l_ref[at, :] = l_ref[at, :] * alpha + part
            a_ref[at, :] = a_ref[at, :] * alpha + jnp.dot(
                p.astype(jnp.bfloat16), v, preferred_element_type=jnp.float32
            )

    @pl.loop(0, spans)
    def _(j):
        here = info[j]

        @pl.when(here < own_span)
        def _():
            fold(j, False)

        @pl.when(here == own_span)
        def _():
            fold(j, True)

    if last:
        total = jnp.sum(l_ref[...], axis=1, keepdims=True)
        out_ref[...] = (a_ref[...] / total).astype(jnp.bfloat16)


def attend(info, q, kv, state, last, rows, heads):
    total_rows, head_size = q.shape
    peers = kv.shape[0]
    vm = pl.BlockSpec(memory_space=pltpu.VMEM)
    stat = jax.ShapeDtypeStruct((total_rows, 128), jnp.float32)
    acc = jax.ShapeDtypeStruct((total_rows, head_size), jnp.float32)
    first = state is None
    args = [info, q, kv] + ([] if first else list(state))
    shapes = [stat, stat, acc]
    if last:
        out_shape = jax.ShapeDtypeStruct((total_rows, head_size), jnp.bfloat16)
        out_specs = vm
        scratch = [pltpu.VMEM(s.shape, s.dtype) for s in shapes]
    else:
        out_shape, out_specs, scratch = shapes, [vm] * 3, []

    def body(*refs):
        attend_kernel(first, last, peers, rows, heads, *refs)

    keys = peers * rows
    return pl.pallas_call(
        body,
        out_shape=out_shape,
        in_specs=[pl.BlockSpec(memory_space=pltpu.SMEM)] + [vm] * (len(args) - 1),
        out_specs=out_specs,
        scratch_shapes=scratch,
        compiler_params=pltpu.CompilerParams(vmem_limit_bytes=40 * 1024 * 1024),
        cost_estimate=pl.CostEstimate(
            flops=4 * total_rows * keys * head_size,
            bytes_accessed=4 * keys * head_size + 2 * total_rows * head_size,
            transcendentals=total_rows * keys,
        ),
    )(*args)


def local(queries, keys, values, span_order):
    rows, heads, head_size = queries.shape
    blk, x, core = lax.axis_index("blk"), lax.axis_index("x"), lax.axis_index("core")
    across = lax.axis_size("blk") * lax.axis_size("x")
    q = queries.reshape(rows * heads, head_size)
    kv = jnp.concatenate([keys.reshape(rows, head_size), values.reshape(rows, head_size)], axis=0)
    place = blk * 2 + x // 2
    own_span = jnp.sum(jnp.where(jnp.arange(16) == place, span_order, 0))
    query_start = (x % 2) * (2 * rows) + core * rows

    def info(which):
        return jnp.concatenate(
            [span_order, jnp.stack([own_span, query_start, which * rows]).astype(jnp.int32)]
        )

    copies = jnp.broadcast_to(kv[None], (across, 2 * rows, head_size))
    mine = lax.all_to_all(copies, ("blk", "x"), 0, 0, tiled=True)
    other = lax.ppermute(mine, "core", [(0, 1), (1, 0)])
    state = attend(info(core), q, mine, None, False, rows, heads)
    out = attend(info(1 - core), q, other, state, True, rows, heads)
    return out.reshape(rows, heads, head_size)


def solution(mesh):
    blk, uly, tp = mesh.devices.shape
    fine = Mesh(mesh.devices.reshape(blk, uly // 2, 2, tp), ("blk", "x", "core", "tp"))
    spec = P(("blk", "x", "core"), "tp", None)
    return jax.shard_map(
        local, mesh=fine, in_specs=(spec, spec, spec, P()), out_specs=spec, check_vma=False
    )
```

time: 264 us -> 92.7 us (0.35)
  the two profiles are of different devices: /device:TPU:1 before, /device:TPU:85 now
where the time goes in v1:
time: 92.7 us; the launch traced here: 92.5 us
  blocking collectives  56.3 us (61%)
  Pallas kernels  29 us (31%)
  starting transfers between devices  4.4 us (5%)
  other arithmetic  2.2 us (2%)
    all_to_all x1, blocking collectives, local(): mine = lax.all_to_all(copies, ('blk', 'x'), 0, 0, tiled=True)  56.3 us
    pallas_call x2, Pallas kernels, attend(): pl.pallas_call(body, out_shape=out_shape, in_specs=[pl.BlockSpec(memory_s...  29 us
    ppermute x1, starting transfers between devices, local(): other = lax.ppermute(mine, 'core', [(0, 1), (1, 0)])  4.4 us
  transfers between devices with their start and end apart: 1, of which 0 were waited for; matrix products, arithmetic and copies ran while one was open for 2% of the time, Pallas kernels for 15%

profile of v1, /device:TPU:85, one launch (start us, length us, event | category | flops | bytes accessed | tf_op | source)
XLA Modules:
  0.0 92.5 jit_solution(14289071338858976638)
XLA Ops:
  0.0 0.8 pad_maximum_fusion
  0.8 0.5 broadcast_in_dim.11
  1.2 0.0 copy-start.1
  1.3 0.0 copy-start
  1.3 56.3 %all_to_all.5.refs_2_ = bf16[32,256,128]{2,1,0:T(8,128)(2,1)S(1)} all-to-all(bf16[32,256,128]{2,1,0:T(8,128)(2,1)S(1)} %broadcast_in_dim.11), channel_id=1, replica_groups=mesh['blk'=8,'x'=4,'core'=2,'tp'=8] {'blk','x'}, dimensions={0} | all-to-all | bytes 4194304 | tf_op jit(solution)/shard_map/all_to_all | solution.py:136
  57.6 4.4 %collective-permute-start = (bf16[32,256,128]{2,1,0:T(8,128)(2,1)S(1)}, bf16[32,256,128]{2,1,0:T(8,128)(2,1)}, u32[]{:S(2)}, u32[]{:S(2)}) collective-permute-start(bf16[32,256,128]{2,1,0:T(8,128)(2,1)S(1)} %all_to_all.5.refs_2_), channel_id=1, source_target_pairs={{0,8},{8,0},{1,9},{9,1},{2,10},{10,2},{3,11},{11,3},{4,12},{12,4},... | collective-permute-start | bytes 6291464 | tf_op jit(solution)/shard_map/ppermute | solution.py:137
  62.1 0.0 copy-done.1
  62.1 0.6 fusion
  62.7 0.7 pad_add_fusion.2
  63.4 0.1 pad_add_fusion.refs_0_
  63.5 0.0 copy-done
  63.5 13.6 %shard_map.46 = (f32[1024,128]{1,0:T(8,128)S(1)}, f32[1024,128]{1,0:T(8,128)S(1)}, f32[1024,128]{1,0:T(8,128)S(1)}) custom-call(s32[19]{0:T(128)S(1)} %get-tuple-element.11.refs_0_, bf16[1024,128]{1,0:T(8,128)(2,1)S(1)} %bitcast.8, bf16[32,256,128]{2,1,0:T(8,128)(2,1)S(1)} %all_to_all.5.refs_2_), custom_call_target="tpu_custom_call" | custom-call | flops 2147483648 | bytes 2359296 | tf_op jit(solution)/shard_map/pallas_call | solution.py:105
  77.1 0.0 collective-permute-done.refs_2_
  77.1 15.3 %shard_map.47 = bf16[1024,128]{1,0:T(8,128)(2,1)} custom-call(s32[19]{0:T(128)S(1)} %pad_add_fusion.refs_0_, bf16[1024,128]{1,0:T(8,128)(2,1)S(1)} %bitcast.9, bf16[32,256,128]{2,1,0:T(8,128)(2,1)} %collective-permute-done.refs_2_, f32[1024,128]{1,0:T(8,128)S(1)} %get-tuple-element.8.refs_3_, f32[1024,128]{1,0:T(8,128)S(1)} %get-tuple-element.9.refs_4_, ...), custom_call_target="tpu_custom_call" | custom-call | flops 2147483648 | bytes 2359296 | tf_op jit(solution)/shard_map/pallas_call | solution.py:105
Async XLA Ops:
  1.2 60.8 %copy-start.1 = (s32[16]{0:T(128)S(1)}, s32[16]{0:T(128)}, u32[]{:S(2)}) copy-start(s32[16]{0:T(128)} %param.7) | copy-start | bytes 196
  1.3 62.2 %copy-start = (bf16[128,8,128]{2,1,0:T(8,128)(2,1)S(1)}, bf16[128,8,128]{2,1,0:T(8,128)(2,1)}, u32[]{:S(2)}) copy-start(bf16[128,8,128]{2,1,0:T(8,128)(2,1)} %param.4) | copy-start | bytes 786436
  57.6 19.5 %collective-permute-start = (bf16[32,256,128]{2,1,0:T(8,128)(2,1)S(1)}, bf16[32,256,128]{2,1,0:T(8,128)(2,1)}, u32[]{:S(2)}, u32[]{:S(2)}) collective-permute-start(bf16[32,256,128]{2,1,0:T(8,128)(2,1)S(1)} %all_to_all.5.refs_2_), channel_id=1, source_target_pairs={{0,8},{8,0},{1,9},{9,1},{2,10},{10,2},{3,11},{11,3},{4,12},{12,4},... | collective-permute-start | bytes 6291464 | tf_op jit(solution)/shard_map/ppermute | solution.py:137

commit v2 on v1

v2 whole, which is shorter than its diff:
```python
import math

import jax
import jax.numpy as jnp
from jax import lax
from jax.experimental import pallas as pl
from jax.experimental.pallas import tpu as pltpu
from jax.sharding import Mesh, PartitionSpec as P

LOG2E = 1.4426950408889634
MASKED = -1.5e38
START = -1.0e30
FAR = 1 << 20
SPANS = 16
GROUP = 8
COLUMNS = 1024
VMEM_BYTES = 40 * 1024 * 1024


def prepare_kernel(q_ref, t_ref):
    head_size = q_ref.shape[1]
    scaled = q_ref[...].astype(jnp.float32).T * (LOG2E / math.sqrt(head_size))
    high = scaled.astype(jnp.bfloat16)
    t_ref[:head_size, :] = high
    t_ref[head_size:, :] = (scaled - high.astype(jnp.float32)).astype(jnp.bfloat16)


def prepare(q):
    vm = pl.BlockSpec(memory_space=pltpu.VMEM)
    return pl.pallas_call(
        prepare_kernel,
        out_shape=jax.ShapeDtypeStruct((2 * q.shape[1], q.shape[0]), q.dtype),
        in_specs=[vm],
        out_specs=vm,
        compiler_params=pltpu.CompilerParams(vmem_limit_bytes=VMEM_BYTES),
    )(q)


def attend_kernel(count, first, last, heads, info, q_ref, kv_ref, *refs):
    if not first:
        m_in, l_in, a_in, *refs = refs
    if last:
        out_ref, m_ref, l_ref, a_ref, seen, base = refs
    else:
        m_ref, l_ref, a_ref, seen, base = refs
    if first:
        m_ref[...] = jnp.full(m_ref.shape, START, jnp.float32)
        l_ref[...] = jnp.zeros(l_ref.shape, jnp.float32)
        a_ref[...] = jnp.zeros(a_ref.shape, jnp.float32)
    else:
        m_ref[...] = m_in[...]
        l_ref[...] = l_in[...]
        a_ref[...] = a_in[...]
    total = q_ref.shape[1]
    rows = kv_ref.shape[1] // 2
    query_start = info[0]

    for i in range(count + GROUP):
        seen[i] = 0
        base[i] = FAR
    free = jnp.int32(0)
    for e in range(count):
        seen[free] = e
        base[free] = -FAR
        free = free + (info[1 + 2 * e] == 1).astype(jnp.int32)
    full = free // GROUP
    for e in range(count):
        own = info[1 + 2 * e] == 2
        seen[free] = e
        base[free] = jnp.where(own, info[2 + 2 * e], FAR)
        free = free + own.astype(jnp.int32)
    base[free] = FAR

    def fold(g, masked):
        blocks = [kv_ref[pl.ds(seen[g * GROUP + i], 1)] for i in range(GROUP)]
        k = jnp.concatenate([b[0, :rows] for b in blocks], axis=0)
        v = jnp.concatenate([b[0, rows:] for b in blocks], axis=0)
        k = jnp.concatenate([k, k], axis=1)
        for c in range(0, total, COLUMNS):
            at = pl.ds(c, COLUMNS)
            s = jnp.dot(k, q_ref[:, at], preferred_element_type=jnp.float32)
            if masked:
                shape = (rows, COLUMNS)
                offset = query_start + (lax.broadcasted_iota(jnp.int32, shape, 1) + c) // heads
                gap = offset - lax.broadcasted_iota(jnp.int32, shape, 0)
                s = jnp.concatenate(
                    [
                        jnp.where(gap >= base[g * GROUP + i], s[i * rows : (i + 1) * rows], MASKED)
                        for i in range(GROUP)
                    ],
                    axis=0,
                )
            m_old = m_ref[:, at]
            m_new = jnp.maximum(m_old, jnp.max(s, axis=0, keepdims=True))
            alpha = jnp.exp2(m_old - m_new)
            p = jnp.exp2(s - m_new)
            m_ref[:, at] = m_new
            l_ref[:, at] = l_ref[:, at] * alpha + jnp.sum(p, axis=0, keepdims=True)
            a_ref[:, at] = a_ref[:, at] * alpha + lax.dot_general(
                v,
                p.astype(jnp.bfloat16),
                (((0,), (0,)), ((), ())),
                preferred_element_type=jnp.float32,
            )

    @pl.loop(0, full)
    def _(g):
        fold(g, False)

    @pl.loop(full, (free + GROUP - 1) // GROUP)
    def _(g):
        fold(g, True)

    if last:
        out_ref[...] = (a_ref[...] / l_ref[...]).T.astype(jnp.bfloat16)


def attend(info, q, kv, state, last, heads):
    total = q.shape[1]
    count, both_rows, head_size = kv.shape
    vm = pl.BlockSpec(memory_space=pltpu.VMEM)
    stat = jax.ShapeDtypeStruct((1, total), jnp.float32)
    acc = jax.ShapeDtypeStruct((head_size, total), jnp.float32)
    first = state is None
    args = [info, q, kv] + ([] if first else list(state))
    shapes = [stat, stat, acc]
    lists = [pltpu.SMEM((count + GROUP + 1,), jnp.int32)] * 2
    if last:
        out_shape = jax.ShapeDtypeStruct((total, head_size), jnp.bfloat16)
        out_specs = vm
        scratch = [pltpu.VMEM(s.shape, s.dtype) for s in shapes] + lists
    else:
        out_shape, out_specs, scratch = shapes, [vm] * 3, lists

    def body(*refs):
        attend_kernel(count, first, last, heads, *refs)

    keys = count * both_rows // 2
    return pl.pallas_call(
        body,
        out_shape=out_shape,
        in_specs=[pl.BlockSpec(memory_space=pltpu.SMEM)] + [vm] * (len(args) - 1),
        out_specs=out_specs,
        scratch_shapes=scratch,
        compiler_params=pltpu.CompilerParams(vmem_limit_bytes=VMEM_BYTES),
        cost_estimate=pl.CostEstimate(
            flops=4 * total * keys * head_size,
            bytes_accessed=4 * keys * head_size + 2 * total * head_size,
            transcendentals=total * keys,
        ),
    )(*args)


def local(queries, keys, values, span_order):
    rows, heads, head_size = queries.shape
    blk, x, core = lax.axis_index("blk"), lax.axis_index("x"), lax.axis_index("core")
    down, across = lax.axis_size("blk"), lax.axis_size("x")
    per_span = across // 2
    q = prepare(queries.reshape(rows * heads, head_size))
    kv = jnp.concatenate([keys.reshape(rows, head_size), values.reshape(rows, head_size)], axis=0)
    hit = jnp.arange(SPANS, dtype=jnp.int32) == 2 * blk + x // per_span
    own_span = jnp.sum(jnp.where(hit, span_order, 0))
    kinds = jnp.where(span_order < own_span, 1, jnp.where(span_order == own_span, 2, 0))
    kinds = kinds.reshape(down, 2).T[jnp.arange(across) // per_span]
    column = jnp.arange(across, dtype=jnp.int32)

    def info(which, columns, kinds):
        starts = (columns % per_span) * (2 * rows) + which * rows
        starts = jnp.broadcast_to(starts[:, None], kinds.shape)
        query_start = (x % per_span) * (2 * rows) + core * rows
        pairs = jnp.stack([kinds, starts], axis=2).reshape(-1)
        return jnp.concatenate([query_start[None], pairs]).astype(jnp.int32)

    here = column == x
    own_kinds = jnp.sum(jnp.where(here[:, None], kinds, 0), axis=0, keepdims=True)
    other_kinds = jnp.where(here[:, None], 0, kinds)
    swap = [(0, 1), (1, 0)]

    copies = jnp.broadcast_to(kv[None], (down, 2 * rows, head_size))
    mine = lax.all_to_all(copies, "blk", 0, 0, tiled=True)
    mine_swapped = lax.ppermute(mine, "core", swap)
    spread = jnp.broadcast_to(mine[None], (across, down, 2 * rows, head_size))
    all_mine = lax.all_to_all(spread, "x", 0, 0, tiled=True)
    all_mine = all_mine.reshape(across * down, 2 * rows, head_size)
    all_swapped = lax.ppermute(all_mine, "core", swap)
    state = attend(info(core, x[None], own_kinds), q, mine, None, False, heads)
    state = attend(info(1 - core, x[None], own_kinds), q, mine_swapped, state, False, heads)
    state = attend(info(core, column, other_kinds), q, all_mine, state, False, heads)
    out = attend(info(1 - core, column, other_kinds), q, all_swapped, state, True, heads)
    return out.reshape(rows, heads, head_size)


def solution(mesh):
    blk, uly, tp = mesh.devices.shape
    fine = Mesh(mesh.devices.reshape(blk, uly // 2, 2, tp), ("blk", "x", "core", "tp"))
    spec = P(("blk", "x", "core"), "tp", None)
    return jax.shard_map(
        local, mesh=fine, in_specs=(spec, spec, spec, P()), out_specs=spec, check_vma=False
    )
```

time: 92.7 us -> 79 us (0.85)
  the two profiles are of different devices: /device:TPU:85 before, /device:TPU:479 now
where the time goes in v2:
time: 79 us; the launch traced here: 78.6 us
  waiting for transfers between devices  21.9 us (28%)
  blocking collectives  19.9 us (25%)
  Pallas kernels  19.6 us (25%)
  starting transfers between devices  11.1 us (14%)
  local copies, waits for them, and re-layouts  3.41 us (4%)
  other arithmetic  2.58 us (3%)
    all_to_all x1, waiting for transfers between devices, local(): all_mine = lax.all_to_all(spread, 'x', 0, 0, tiled=True)  21.9 us
    all_to_all x1, blocking collectives, local(): mine = lax.all_to_all(copies, 'blk', 0, 0, tiled=True)  19.9 us
    pallas_call x4, Pallas kernels, attend(): pl.pallas_call(body, out_shape=out_shape, in_specs=[pl.BlockSpec(memory_s...  19.4 us
    ppermute x1, starting transfers between devices, local(): all_swapped = lax.ppermute(all_mine, 'core', swap)  4.85 us
    all_to_all x1, starting transfers between devices, local(): all_mine = lax.all_to_all(spread, 'x', 0, 0, tiled=True)  4.34 us
    ppermute x1, starting transfers between devices, local(): mine_swapped = lax.ppermute(mine, 'core', swap)  1.91 us
    broadcast_in_dim x1, local copies, waits for them, and re-layouts, local(): spread = jnp.broadcast_to(mine[None], (across, down, 2 * rows, head_size))  1.81 us
  transfers between devices with their start and end apart: 3, of which 1 were waited for; matrix products, arithmetic and copies ran while one was open for 4% of the time, Pallas kernels for 15%

profile of v2, /device:TPU:479, one launch (start us, length us, event | category | flops | bytes accessed | tf_op | source)
XLA Modules:
  0.0 78.6 jit_solution(8599163431018758745)
XLA Ops:
  0.0 0.8 pad_maximum_fusion
  0.9 19.9 %all_to_all.10.refs_2_ = bf16[8,256,128]{2,1,0:T(8,128)(2,1)S(1)} all-to-all(bf16[8,256,128]{2,1,0:T(8,128)(2,1)S(1)} %broadcast_in_dim.73), channel_id=1, replica_groups=mesh['blk'=8,'x'=4,'core'=2,'tp'=8] {'blk'}, dimensions={0} | all-to-all | bytes 1048576 | tf_op jit(solution)/shard_map/all_to_all | solution.py:180
  20.8 1.8 %broadcast_in_dim.74 = bf16[4,8,256,128]{3,2,1,0:T(8,128)(2,1)} broadcast(bf16[8,256,128]{2,1,0:T(8,128)(2,1)S(1)} %all_to_all.10.refs_2_), dimensions={1,2,3} | broadcast | bytes 2621440 | tf_op jit(solution)/shard_map/broadcast_in_dim | solution.py:182
  22.6 4.3 %all-to-all-start.1 = ((bf16[4,8,256,128]{3,2,1,0:T(8,128)(2,1)}), bf16[4,8,256,128]{3,2,1,0:T(8,128)(2,1)S(1)}, u32[]{:S(2)}, u32[]{:S(2)}) async-start(bf16[4,8,256,128]{3,2,1,0:T(8,128)(2,1)} %broadcast_in_dim.74), calls=%async_computation.1 | async-start | bytes 4194304 | tf_op jit(solution)/shard_map/all_to_all | solution.py:183
  26.9 0.7 fusion.1
  27.6 21.9 %all-to-all-done.1 = bf16[4,8,256,128]{3,2,1,0:T(8,128)(2,1)S(1)} async-done(((bf16[4,8,256,128]{3,2,1,0:T(8,128)(2,1)}), bf16[4,8,256,128]{3,2,1,0:T(8,128)(2,1)S(1)}, u32[]{:S(2)}, u32[]{:S(2)}) %all-to-all-start.1) | async-done | bytes 2097184 | tf_op jit(solution)/shard_map/all_to_all | solution.py:183
  49.5 4.9 %collective-permute-start = (bf16[32,256,128]{2,1,0:T(8,128)(2,1)S(1)}, bf16[32,256,128]{2,1,0:T(8,128)(2,1)}, u32[]{:S(2)}, u32[]{:S(2)}) collective-permute-start(bf16[32,256,128]{2,1,0:T(8,128)(2,1)S(1)} %bitcast.17), channel_id=1, source_target_pairs={{0,8},{8,0},{1,9},{9,1},{2,10},{10,2},{3,11},{11,3},{4,12},{12,4},... | collective-permute-start | bytes 6291464 | tf_op jit(solution)/shard_map/ppermute | solution.py:185
  54.3 0.6 compare_select_fusion.2
  55.1 0.1 copy.10
  55.2 0.6 gather_fusion
  55.7 0.1 select_reduce_fusion
  55.8 0.1 copy.15
  56.1 1.9 %collective-permute-start.1 = (bf16[8,256,128]{2,1,0:T(8,128)(2,1)S(1)}, bf16[8,256,128]{2,1,0:T(8,128)(2,1)S(1)}, u32[]{:S(2)}, u32[]{:S(2)}) collective-permute-start(bf16[8,256,128]{2,1,0:T(8,128)(2,1)S(1)} %all_to_all.10.refs_2_), channel_id=1, source_target_pairs={{0,8},{8,0},{1,9},{9,1},{2,10},{10,2},{3,11},{11,3},{4,12},{12,4},... | collective-permute-start | bytes 1572872 | tf_op jit(solution)/shard_map/ppermute | solution.py:181
  58.1 0.1 reshape.119
  58.2 0.1 reshape.118
  58.2 0.1 copy.12
  58.3 0.1 reshape.117
  58.5 0.1 copy.11
  58.5 0.1 reshape.112
  58.7 0.2 shard_map.46.refs_1_
  59.1 2.4 %shard_map.47 = (f32[1,1024]{1,0:T(1,128)S(1)}, f32[1,1024]{1,0:T(1,128)S(1)}, f32[128,1024]{1,0:T(8,128)S(1)}) custom-call(s32[17]{0:T(128)S(1)} %pad_add_fusion.5.refs_0_, bf16[256,1024]{1,0:T(8,128)(2,1)S(1)} %shard_map.46.refs_1_, bf16[8,256,128]{2,1,0:T(8,128)(2,1)S(1)} %all_to_all.10.refs_2_), custom_call_target="tpu_custom_call" | custom-call | flops 536870912 | bytes 786432 | tf_op jit(solution)/shard_map/pallas_call | solution.py:139
  61.6 2.4 %shard_map.48 = (f32[1,1024]{1,0:T(1,128)S(1)}, f32[1,1024]{1,0:T(1,128)S(1)}, f32[128,1024]{1,0:T(8,128)S(1)}) custom-call(s32[17]{0:T(128)S(1)} %pad_add_fusion.4.refs_0_, bf16[256,1024]{1,0:T(8,128)(2,1)S(1)} %shard_map.46.refs_1_, bf16[8,256,128]{2,1,0:T(8,128)(2,1)S(1)} %collective-permute-done.1.refs_2_, f32[1,1024]{1,0:T(1,128)S(1)} %get-tuple-element.14.refs_3_, ...), custom_call_target="tpu_custom_call" | custom-call | flops 536870912 | bytes 786432 | tf_op jit(solution)/shard_map/pallas_call | solution.py:139
  64.0 6.4 %shard_map.49 = (f32[1,1024]{1,0:T(1,128)S(1)}, f32[1,1024]{1,0:T(1,128)S(1)}, f32[128,1024]{1,0:T(8,128)S(1)}) custom-call(s32[65]{0:T(128)S(1)} %pad_add_fusion.3.refs_0_, bf16[256,1024]{1,0:T(8,128)(2,1)S(1)} %shard_map.46.refs_1_, bf16[32,256,128]{2,1,0:T(8,128)(2,1)S(1)} %bitcast.18, f32[1,1024]{1,0:T(1,128)S(1)} %get-tuple-element.17.refs_3_, ...), custom_call_target="tpu_custom_call" | custom-call | flops 2147483648 | bytes 2359296 | tf_op jit(solution)/shard_map/pallas_call | solution.py:139
  70.5 8.2 %shard_map.50 = bf16[1024,128]{1,0:T(8,128)(2,1)} custom-call(s32[65]{0:T(128)S(1)} %pad_add_fusion.2.refs_0_, bf16[256,1024]{1,0:T(8,128)(2,1)S(1)} %shard_map.46.refs_1_, bf16[32,256,128]{2,1,0:T(8,128)(2,1)} %collective-permute-done.refs_2_, f32[1,1024]{1,0:T(1,128)S(1)} %get-tuple-element.20.refs_3_, f32[1,1024]{1,0:T(1,128)S(1)} %get-tuple-element.21.refs_4_, ...), custom_call_target="tpu_custom_call" | custom-call | flops 2147483648 | bytes 2359296 | tf_op jit(solution)/shard_map/pallas_call | solution.py:139
  (22 shorter events, 0.7 us)
Async XLA Ops:
  22.6 4.3 %copy-start.1 = (s32[16]{0:T(128)S(1)}, s32[16]{0:T(128)}, u32[]{:S(2)}) copy-start(s32[16]{0:T(128)} %param.7) | copy-start | bytes 196
  22.6 36.1 %copy-start = (bf16[128,8,128]{2,1,0:T(8,128)(2,1)S(1)}, bf16[128,8,128]{2,1,0:T(8,128)(2,1)}, u32[]{:S(2)}) copy-start(bf16[128,8,128]{2,1,0:T(8,128)(2,1)} %param.4) | copy-start | bytes 786436
  22.6 26.9 %all-to-all-start.1 = ((bf16[4,8,256,128]{3,2,1,0:T(8,128)(2,1)}), bf16[4,8,256,128]{3,2,1,0:T(8,128)(2,1)S(1)}, u32[]{:S(2)}, u32[]{:S(2)}) async-start(bf16[4,8,256,128]{3,2,1,0:T(8,128)(2,1)} %broadcast_in_dim.74), calls=%async_computation.1 | async-start | bytes 4194304 | tf_op jit(solution)/shard_map/all_to_all | solution.py:183
  49.5 21.0 %collective-permute-start = (bf16[32,256,128]{2,1,0:T(8,128)(2,1)S(1)}, bf16[32,256,128]{2,1,0:T(8,128)(2,1)}, u32[]{:S(2)}, u32[]{:S(2)}) collective-permute-start(bf16[32,256,128]{2,1,0:T(8,128)(2,1)S(1)} %bitcast.17), channel_id=1, source_target_pairs={{0,8},{8,0},{1,9},{9,1},{2,10},{10,2},{3,11},{11,3},{4,12},{12,4},... | collective-permute-start | bytes 6291464 | tf_op jit(solution)/shard_map/ppermute | solution.py:185
  56.1 5.5 %collective-permute-start.1 = (bf16[8,256,128]{2,1,0:T(8,128)(2,1)S(1)}, bf16[8,256,128]{2,1,0:T(8,128)(2,1)S(1)}, u32[]{:S(2)}, u32[]{:S(2)}) collective-permute-start(bf16[8,256,128]{2,1,0:T(8,128)(2,1)S(1)} %all_to_all.10.refs_2_), channel_id=1, source_target_pairs={{0,8},{8,0},{1,9},{9,1},{2,10},{10,2},{3,11},{11,3},{4,12},{12,4},... | collective-permute-start | bytes 1572872 | tf_op jit(solution)/shard_map/ppermute | solution.py:181

commit v3 on v2

v3 whole, which is shorter than its diff:
```python
import math

import jax
import jax.numpy as jnp
from jax import lax
from jax.experimental import pallas as pl
from jax.experimental.pallas import tpu as pltpu
from jax.sharding import Mesh, PartitionSpec as P

LOG2E = 1.4426950408889634
MASKED = -1.5e38
START = -1.0e30
FAR = 1 << 20
COLUMNS = 1024
VMEM_BYTES = 40 * 1024 * 1024
VM = pl.BlockSpec(memory_space=pltpu.VMEM)
SM = pl.BlockSpec(memory_space=pltpu.SMEM)
PARAMS = pltpu.CompilerParams(vmem_limit_bytes=VMEM_BYTES)


def split(x):
    high = x.astype(jnp.bfloat16)
    return high, x - high.astype(jnp.float32)


def prepare_kernel(q_ref, other_ref, t_ref):
    total, head_size = q_ref.shape
    for i, ref in enumerate((q_ref, other_ref)):
        scaled = ref[...].astype(jnp.float32).T * (LOG2E / math.sqrt(head_size))
        high, rest = split(scaled)
        t_ref[:head_size, i * total : (i + 1) * total] = high
        t_ref[head_size:, i * total : (i + 1) * total] = rest.astype(jnp.bfloat16)


def prepare(q, other):
    return pl.pallas_call(
        prepare_kernel,
        out_shape=jax.ShapeDtypeStruct((2 * q.shape[1], 2 * q.shape[0]), q.dtype),
        in_specs=[VM, VM],
        out_specs=VM,
        compiler_params=PARAMS,
    )(q, other)


def attend_kernel(shifts, down, first, last, heads, order, q_ref, *refs):
    pieces, refs = refs[: len(shifts)], refs[len(shifts) :]
    if not first:
        m_in, l_in, a_in, *refs = refs
    if last:
        m_out, l_out, a_out, p_out, m_ref, l_ref, a_ref, kv_ref, base = refs
    else:
        m_ref, l_ref, a_ref, kv_ref, base = refs
    if first:
        m_ref[...] = jnp.full(m_ref.shape, START, jnp.float32)
        l_ref[...] = jnp.zeros(l_ref.shape, jnp.float32)
        a_ref[...] = jnp.zeros(a_ref.shape, jnp.float32)
    else:
        m_ref[...] = m_in[...]
        l_ref[...] = l_in[...]
        a_ref[...] = a_in[...]
    depth, total = a_ref.shape
    mine = total // 2
    across, both_rows, _ = pieces[0].shape
    rows = both_rows // 2
    count = across * len(shifts)
    per_span = across // 2
    blk, x, core = lax.axis_index("blk"), lax.axis_index("x"), lax.axis_index("core")
    own_span = order[2 * blk + x // per_span]
    place = (x % per_span) * both_rows

    for i in range(count):
        base[i] = FAR
    free = jnp.int32(0)
    for kind in (1, 2):
        for piece, shift in zip(pieces, shifts):
            row = lax.rem(blk + (down - shift), down)
            for column in range(across):
                here = order[2 * row + column // per_span]
                start = (column % per_span) * both_rows + core * rows
                chosen = here < own_span if kind == 1 else here == own_span
                if kind == 2 and shift != 0:
                    continue

                @pl.when(chosen)
                def _():
                    kv_ref[pl.ds(free, 1)] = piece[column : column + 1]
                    base[free] = -FAR if kind == 1 else start

                free = free + chosen.astype(jnp.int32)
        if kind == 1:
            visible = free

    def fold(group, masked):
        blocks = [kv_ref[i] for i in range(group)]
        k = jnp.concatenate([b[:rows] for b in blocks], axis=0)
        v = jnp.concatenate([b[rows:] for b in blocks], axis=0)
        k = jnp.concatenate([k, k], axis=1)
        parts = range(0, total, COLUMNS)
        scores = [
            jnp.dot(k, q_ref[:, c : c + COLUMNS], preferred_element_type=jnp.float32) for c in parts
        ]
        for c, s in zip(parts, scores):
            at = pl.ds(c, COLUMNS)
            if masked:
                shape = (rows, COLUMNS)
                lane = lax.broadcasted_iota(jnp.int32, shape, 1) + c % mine
                query_core = core if c < mine else 1 - core
                gap = place + query_core * rows + lane // heads - lax.broadcasted_iota(jnp.int32, shape, 0)
                s = jnp.concatenate(
                    [
                        jnp.where(gap >= base[i], s[i * rows : (i + 1) * rows], MASKED)
                        for i in range(group)
                    ],
                    axis=0,
                )
            m_old = m_ref[:, at]
            m_new = jnp.maximum(m_old, jnp.max(s, axis=0, keepdims=True))
            alpha = jnp.exp2(m_old - m_new)
            p = jnp.exp2(s - m_new)
            m_ref[:, at] = m_new
            l_ref[:, at] = l_ref[:, at] * alpha + jnp.sum(p, axis=0, keepdims=True)
            a_ref[:, at] = a_ref[:, at] * alpha + lax.dot_general(
                v,
                p.astype(jnp.bfloat16),
                (((0,), (0,)), ((), ())),
                preferred_element_type=jnp.float32,
            )

    @pl.when(visible == count)
    def _():
        fold(count, False)

    if count > 4:

        @pl.when((visible < count) & (free > 4))
        def _():
            for i in range(4, count):

                @pl.when(i >= free)
                def _():
                    kv_ref[i] = jnp.zeros(kv_ref.shape[1:], kv_ref.dtype)

            fold(count, True)

    @pl.when((visible < count) & (free > 0) & (free <= 4))
    def _():
        for i in range(1, 4):

            @pl.when(i >= free)
            def _():
                kv_ref[i] = jnp.zeros(kv_ref.shape[1:], kv_ref.dtype)

        fold(4, True)

    if last:
        m_out[...] = m_ref[:, :mine]
        l_out[...] = l_ref[:, :mine]
        a_out[...] = a_ref[:, :mine]
        l = l_ref[:, mine:]
        some = l > 0.0
        p_out[:depth, :] = (a_ref[:, mine:] / jnp.where(some, l, 1.0)).astype(jnp.bfloat16)
        level = jnp.where(some, m_ref[:, mine:] + jnp.log(jnp.where(some, l, 1.0)) * LOG2E, START)
        high, rest = split(level)
        mid, rest = split(rest)
        line = lax.broadcasted_iota(jnp.int32, (p_out.shape[0] - depth, mine), 0)
        packed = jnp.where(
            line == 0,
            high.astype(jnp.float32),
            jnp.where(line == 1, mid.astype(jnp.float32), jnp.where(line == 2, rest, 0.0)),
        )
        p_out[depth:, :] = packed.astype(jnp.bfloat16)


def attend(order, q, pieces, shifts, state, last, heads, down):
    total = q.shape[1]
    across, both_rows, head_size = pieces[0].shape
    count = across * len(pieces)
    first = state is None
    args = [order, q] + list(pieces) + ([] if first else list(state))

    def shapes(n):
        stat = jax.ShapeDtypeStruct((1, n), jnp.float32)
        return [stat, stat, jax.ShapeDtypeStruct((head_size, n), jnp.float32)]

    extra = [
        pltpu.VMEM((count, both_rows, head_size), jnp.bfloat16),
        pltpu.SMEM((count + 1,), jnp.int32),
    ]
    if last:
        packet = jax.ShapeDtypeStruct((head_size + 16, total // 2), jnp.bfloat16)
        out_shape = shapes(total // 2) + [packet]
        scratch = [pltpu.VMEM(s.shape, s.dtype) for s in shapes(total)] + extra
    else:
        out_shape, scratch = shapes(total), extra

    def body(*refs):
        attend_kernel(shifts, down, first, last, heads, *refs)

    keys = count * both_rows // 2
    return pl.pallas_call(
        body,
        out_shape=out_shape,
        in_specs=[SM] + [VM] * (len(args) - 1),
        out_specs=[VM] * len(out_shape),
        scratch_shapes=scratch,
        compiler_params=PARAMS,
        cost_estimate=pl.CostEstimate(
            flops=4 * total * keys * head_size,
            bytes_accessed=4 * keys * head_size + 2 * total * head_size,
            transcendentals=total * keys,
        ),
    )(*args)


def combine_kernel(m_ref, l_ref, a_ref, p_ref, out_ref):
    depth = a_ref.shape[0]
    level = (
        p_ref[depth : depth + 1].astype(jnp.float32)
        + p_ref[depth + 1 : depth + 2].astype(jnp.float32)
        + p_ref[depth + 2 : depth + 3].astype(jnp.float32)
    )
    top = jnp.maximum(m_ref[...], level)
    here, there = jnp.exp2(m_ref[...] - top), jnp.exp2(level - top)
    whole = 1.0 / (l_ref[...] * here + there)
    mixed = a_ref[...] * (here * whole) + p_ref[:depth].astype(jnp.float32) * (there * whole)
    out_ref[...] = mixed.T.astype(jnp.bfloat16)


def combine(m, l, a, packet):
    return pl.pallas_call(
        combine_kernel,
        out_shape=jax.ShapeDtypeStruct(a.shape[::-1], jnp.bfloat16),
        in_specs=[VM] * 4,
        out_specs=VM,
        compiler_params=PARAMS,
    )(m, l, a, packet)


def local(queries, keys, values, span_order):
    rows, heads, head_size = queries.shape
    down, across = lax.axis_size("blk"), lax.axis_size("x")
    swap = [(0, 1), (1, 0)]
    own = queries.reshape(rows * heads, head_size)
    other = lax.ppermute(own, "core", swap)
    kv = jnp.concatenate([keys.reshape(rows, head_size), values.reshape(rows, head_size)], axis=0)
    copies = jnp.broadcast_to(kv[None], (across, 2 * rows, head_size))
    row = lax.all_to_all(copies, "x", 0, 0, tiled=True)
    up = [(i, (i + 1) % down) for i in range(down)]
    back = [(i, (i - 1) % down) for i in range(down)]
    q = prepare(own, other)
    state = attend(span_order, q, [row], [0], None, False, heads, down)
    rising = falling = row
    for hop in range(1, down // 2):
        rising = lax.ppermute(rising, "blk", up)
        falling = lax.ppermute(falling, "blk", back)
        state = attend(
            span_order, q, [rising, falling], [hop, down - hop], state, False, heads, down
        )
    rising = lax.ppermute(rising, "blk", up)
    m, l, a, packet = attend(span_order, q, [rising], [down // 2], state, True, heads, down)
    packet = lax.ppermute(packet, "core", swap)
    return combine(m, l, a, packet).reshape(rows, heads, head_size)


def solution(mesh):
    blk, uly, tp = mesh.devices.shape
    fine = Mesh(mesh.devices.reshape(blk, uly // 2, 2, tp), ("blk", "x", "core", "tp"))
    spec = P(("blk", "x", "core"), "tp", None)
    return jax.shard_map(
        local, mesh=fine, in_specs=(spec, spec, spec, P()), out_specs=spec, check_vma=False
    )
```

time: 79 us -> 69.8 us (0.88)
  the two profiles are of different devices: /device:TPU:479 before, /device:TPU:57 now
where the time goes in v3:
time: 69.8 us; the launch traced here: 69.3 us
  starting transfers between devices  34 us (49%)
  Pallas kernels  20.7 us (30%)
  blocking collectives  9.5 us (14%)
  waiting for transfers between devices  4.12 us (6%)
  other arithmetic  0.78 us (1%)
    pallas_call x5, Pallas kernels, attend(): pl.pallas_call(body, out_shape=out_shape, in_specs=[SM] + [VM] * (len(arg...  19.6 us
    ppermute x4, starting transfers between devices, local(): rising = lax.ppermute(rising, 'blk', up)  14.7 us
    all_to_all x1, blocking collectives, local(): row = lax.all_to_all(copies, 'x', 0, 0, tiled=True)  9.5 us
    ppermute x1, starting transfers between devices, local(): other = lax.ppermute(own, 'core', swap)  8.19 us
    ppermute x3, starting transfers between devices, local(): falling = lax.ppermute(falling, 'blk', back)  7.93 us
    ppermute x1, starting transfers between devices, local(): packet = lax.ppermute(packet, 'core', swap)  3.16 us
    ppermute x4, waiting for transfers between devices, local(): rising = lax.ppermute(rising, 'blk', up)  2.91 us
  transfers between devices with their start and end apart: 9, of which 3 were waited for; matrix products, arithmetic and copies ran while one was open for 0% of the time, Pallas kernels for 25%

profile of v3, /device:TPU:57, one launch (start us, length us, event | category | flops | bytes accessed | tf_op | source)
XLA Modules:
  0.0 69.3 jit_solution(11959271834159891045)
XLA Ops:
  0.0 0.8 %pad_maximum_fusion = bf16[256,128]{1,0:T(8,128)(2,1)S(1)} fusion(bf16[128,128]{1,0:T(8,128)(2,1)} %bitcast.6, bf16[128,128]{1,0:T(8,128)(2,1)} %bitcast.7), kind=kLoop, calls=%fused_computation | loop fusion | flops 131072 | bytes 131072 | tf_op jit(solution)/shard_map/concatenate | solution.py:245
  0.8 0.0 copy-start
  0.8 9.5 %all_to_all.5.refs_2_ = bf16[4,256,128]{2,1,0:T(8,128)(2,1)S(1)} all-to-all(bf16[4,256,128]{2,1,0:T(8,128)(2,1)S(1)} %broadcast_in_dim.2), channel_id=1, replica_groups=mesh['blk'=8,'x'=4,'core'=2,'tp'=8] {'x'}, dimensions={0} | all-to-all | bytes 524288 | tf_op jit(solution)/shard_map/all_to_all | solution.py:247
  10.3 1.9 %collective-permute-start.1 = (bf16[4,256,128]{2,1,0:T(8,128)(2,1)S(1)}, bf16[4,256,128]{2,1,0:T(8,128)(2,1)S(1)}, u32[]{:S(2)}, u32[]{:S(2)}) collective-permute-start(bf16[4,256,128]{2,1,0:T(8,128)(2,1)S(1)} %all_to_all.5.refs_2_), channel_id=1, source_target_pairs={{0,64},{64,128},{128,192},{192,256},{256,320},{320,384},{384,448},... | collective-permute-start | bytes 786440 | tf_op jit(solution)/shard_map/ppermute | solution.py:254
  12.2 3.4 %collective-permute-start.5 = (bf16[4,256,128]{2,1,0:T(8,128)(2,1)S(1)}, bf16[4,256,128]{2,1,0:T(8,128)(2,1)S(1)}, u32[]{:S(2)}, u32[]{:S(2)}) collective-permute-start(bf16[4,256,128]{2,1,0:T(8,128)(2,1)S(1)} %all_to_all.5.refs_2_), channel_id=1, source_target_pairs={{0,448},{64,0},{128,64},{192,128},{256,192},{320,256},{384,320},{4... | collective-permute-start | bytes 786440 | tf_op jit(solution)/shard_map/ppermute | solution.py:255
  15.6 2.3 %collective-permute-done.1.refs_2_ = bf16[4,256,128]{2,1,0:T(8,128)(2,1)S(1)} collective-permute-done((bf16[4,256,128]{2,1,0:T(8,128)(2,1)S(1)}, bf16[4,256,128]{2,1,0:T(8,128)(2,1)S(1)}, u32[]{:S(2)}, u32[]{:S(2)}) %collective-permute-start.1) | collective-permute-done | bytes 262176 | tf_op jit(solution)/shard_map/ppermute | solution.py:254
  17.9 2.6 %collective-permute-start.2 = (bf16[4,256,128]{2,1,0:T(8,128)(2,1)S(1)}, bf16[4,256,128]{2,1,0:T(8,128)(2,1)S(1)}, u32[]{:S(2)}, u32[]{:S(2)}) collective-permute-start(bf16[4,256,128]{2,1,0:T(8,128)(2,1)S(1)} %collective-permute-done.1.refs_2_), channel_id=1, source_target_pairs={{0,64},{64,128},{128,192},{192,256},{256,320},{320,384},{384,448},... | collective-permute-start | bytes 786440 | tf_op jit(solution)/shard_map/ppermute | solution.py:254
  20.6 0.0 collective-permute-done.5.refs_3_
  20.6 2.6 %collective-permute-start.6 = (bf16[4,256,128]{2,1,0:T(8,128)(2,1)S(1)}, bf16[4,256,128]{2,1,0:T(8,128)(2,1)S(1)}, u32[]{:S(2)}, u32[]{:S(2)}) collective-permute-start(bf16[4,256,128]{2,1,0:T(8,128)(2,1)S(1)} %collective-permute-done.5.refs_3_), channel_id=1, source_target_pairs={{0,448},{64,0},{128,64},{192,128},{256,192},{320,256},{384,320},{4... | collective-permute-start | bytes 786440 | tf_op jit(solution)/shard_map/ppermute | solution.py:255
  23.2 0.0 copy-start.1
  23.3 8.2 %collective-permute-start = (bf16[1024,128]{1,0:T(8,128)(2,1)S(1)}, bf16[1024,128]{1,0:T(8,128)(2,1)S(1)}, u32[]{:S(2)}, u32[]{:S(2)}) collective-permute-start(bf16[1024,128]{1,0:T(8,128)(2,1)S(1)} %bitcast.4), channel_id=1, source_target_pairs={{0,8},{8,0},{1,9},{9,1},{2,10},{10,2},{3,11},{11,3},{4,12},{12,4},... | collective-permute-start | bytes 786440 | tf_op jit(solution)/shard_map/ppermute | solution.py:244
  31.5 4.9 %collective-permute-start.3 = (bf16[4,256,128]{2,1,0:T(8,128)(2,1)S(1)}, bf16[4,256,128]{2,1,0:T(8,128)(2,1)S(1)}, u32[]{:S(2)}, u32[]{:S(2)}) collective-permute-start(bf16[4,256,128]{2,1,0:T(8,128)(2,1)S(1)} %collective-permute-done.2.refs_2_), channel_id=1, source_target_pairs={{0,64},{64,128},{128,192},{192,256},{256,320},{320,384},{384,448},... | collective-permute-start | bytes 786440 | tf_op jit(solution)/shard_map/ppermute | solution.py:254
  36.3 1.9 %collective-permute-start.7 = (bf16[4,256,128]{2,1,0:T(8,128)(2,1)S(1)}, bf16[4,256,128]{2,1,0:T(8,128)(2,1)S(1)}, u32[]{:S(2)}, u32[]{:S(2)}) collective-permute-start(bf16[4,256,128]{2,1,0:T(8,128)(2,1)S(1)} %collective-permute-done.6.refs_3_), channel_id=1, source_target_pairs={{0,448},{64,0},{128,64},{192,128},{256,192},{320,256},{384,320},{4... | collective-permute-start | bytes 786440 | tf_op jit(solution)/shard_map/ppermute | solution.py:255
  38.3 0.3 shard_map.46.refs_1_
  38.6 2.7 %shard_map.47 = (f32[1,2048]{1,0:T(1,128)S(1)}, f32[1,2048]{1,0:T(1,128)S(1)}, f32[128,2048]{1,0:T(8,128)S(1)}) custom-call(s32[16]{0:T(128)S(1)} %copy-done.1, bf16[256,2048]{1,0:T(8,128)(2,1)S(1)} %shard_map.46.refs_1_, bf16[4,256,128]{2,1,0:T(8,128)(2,1)S(1)} %all_to_all.5.refs_2_), custom_call_target="tpu_custom_call" | custom-call | flops 536870912 | bytes 786432 | tf_op jit(solution)/shard_map/pallas_call | solution.py:200
  41.2 0.6 collective-permute-done.3.refs_2_
  41.8 5.3 %collective-permute-start.4 = (bf16[4,256,128]{2,1,0:T(8,128)(2,1)S(1)}, bf16[4,256,128]{2,1,0:T(8,128)(2,1)S(1)}, u32[]{:S(2)}, u32[]{:S(2)}) collective-permute-start(bf16[4,256,128]{2,1,0:T(8,128)(2,1)S(1)} %collective-permute-done.3.refs_2_), channel_id=1, source_target_pairs={{0,64},{64,128},{128,192},{192,256},{256,320},{320,384},{384,448},... | collective-permute-start | bytes 786440 | tf_op jit(solution)/shard_map/ppermute | solution.py:259
  47.2 4.7 %shard_map.48 = (f32[1,2048]{1,0:T(1,128)S(1)}, f32[1,2048]{1,0:T(1,128)S(1)}, f32[128,2048]{1,0:T(8,128)S(1)}) custom-call(s32[16]{0:T(128)S(1)} %copy-done.1, bf16[256,2048]{1,0:T(8,128)(2,1)S(1)} %shard_map.46.refs_1_, bf16[4,256,128]{2,1,0:T(8,128)(2,1)S(1)} %collective-permute-done.1.refs_2_, bf16[4,256,128]{2,1,0:T(8,128)(2,1)S(1)} %collective-permute-done.5.refs_3_, ...), custom_call_target="tpu_custom_call" | custom-call | flops 1073741824 | bytes 1048576 | tf_op jit(solution)/shard_map/pallas_call | solution.py:200
  51.9 4.5 %shard_map.49 = (f32[1,2048]{1,0:T(1,128)S(1)}, f32[1,2048]{1,0:T(1,128)S(1)}, f32[128,2048]{1,0:T(8,128)S(1)}) custom-call(s32[16]{0:T(128)S(1)} %copy-done.1, bf16[256,2048]{1,0:T(8,128)(2,1)S(1)} %shard_map.46.refs_1_, bf16[4,256,128]{2,1,0:T(8,128)(2,1)S(1)} %collective-permute-done.2.refs_2_, bf16[4,256,128]{2,1,0:T(8,128)(2,1)S(1)} %collective-permute-done.6.refs_3_, ...), custom_call_target="tpu_custom_call" | custom-call | flops 1073741824 | bytes 1048576 | tf_op jit(solution)/shard_map/pallas_call | solution.py:200
  56.4 4.9 %shard_map.50 = (f32[1,2048]{1,0:T(1,128)S(1)}, f32[1,2048]{1,0:T(1,128)S(1)}, f32[128,2048]{1,0:T(8,128)S(1)}) custom-call(s32[16]{0:T(128)S(1)} %copy-done.1, bf16[256,2048]{1,0:T(8,128)(2,1)S(1)} %shard_map.46.refs_1_, bf16[4,256,128]{2,1,0:T(8,128)(2,1)S(1)} %collective-permute-done.3.refs_2_, bf16[4,256,128]{2,1,0:T(8,128)(2,1)S(1)} %collective-permute-done.7.refs_3_, ...), custom_call_target="tpu_custom_call" | custom-call | flops 1073741824 | bytes 1048576 | tf_op jit(solution)/shard_map/pallas_call | solution.py:200
  61.3 2.7 %shard_map.51 = (f32[1,1024]{1,0:T(1,128)S(1)}, f32[1,1024]{1,0:T(1,128)S(1)}, f32[128,1024]{1,0:T(8,128)S(1)}, bf16[144,1024]{1,0:T(8,128)(2,1)S(1)}) custom-call(s32[16]{0:T(128)S(1)} %copy-done.1, bf16[256,2048]{1,0:T(8,128)(2,1)S(1)} %shard_map.46.refs_1_, bf16[4,256,128]{2,1,0:T(8,128)(2,1)S(1)} %collective-permute-done.4.refs_2_, ...), custom_call_target="tpu_custom_call" | custom-call | flops 536870912 | bytes 786432 | tf_op jit(solution)/shard_map/pallas_call | solution.py:200
  64.1 3.2 %collective-permute-start.8 = (bf16[144,1024]{1,0:T(8,128)(2,1)S(1)}, bf16[144,1024]{1,0:T(8,128)(2,1)S(1)}, u32[]{:S(2)}, u32[]{:S(2)}) collective-permute-start(bf16[144,1024]{1,0:T(8,128)(2,1)S(1)} %get-tuple-element.36), channel_id=1, source_target_pairs={{0,8},{8,0},{1,9},{9,1},{2,10},{10,2},{3,11},{11,3},{4,12},{12,4},... | collective-permute-start | bytes 884744 | tf_op jit(solution)/shard_map/ppermute | solution.py:261
  67.3 1.2 %collective-permute-done.8.p_ref = bf16[144,1024]{1,0:T(8,128)(2,1)S(1)} collective-permute-done((bf16[144,1024]{1,0:T(8,128)(2,1)S(1)}, bf16[144,1024]{1,0:T(8,128)(2,1)S(1)}, u32[]{:S(2)}, u32[]{:S(2)}) %collective-permute-start.8) | collective-permute-done | bytes 294944 | tf_op jit(solution)/shard_map/ppermute | solution.py:261
  68.4 0.9 %shard_map.52 = bf16[1024,128]{1,0:T(8,128)(2,1)} custom-call(f32[1,1024]{1,0:T(1,128)S(1)} %get-tuple-element.33.m_ref, f32[1,1024]{1,0:T(1,128)S(1)} %get-tuple-element.34.l_ref, f32[128,1024]{1,0:T(8,128)S(1)} %get-tuple-element.35.a_ref, bf16[144,1024]{1,0:T(8,128)(2,1)S(1)} %collective-permute-done.8.p_ref), custom_call_target="tpu_custom_call" | custom-call | tf_op jit(solution)/shard_map/pallas_call | solution.py:230
  (8 shorter events, 0.1 us)
Async XLA Ops:
  0.8 22.4 %copy-start = (bf16[128,8,128]{2,1,0:T(8,128)(2,1)S(1)}, bf16[128,8,128]{2,1,0:T(8,128)(2,1)}, u32[]{:S(2)}) copy-start(bf16[128,8,128]{2,1,0:T(8,128)(2,1)} %param.4) | copy-start | bytes 786436
  10.3 7.6 %collective-permute-start.1 = (bf16[4,256,128]{2,1,0:T(8,128)(2,1)S(1)}, bf16[4,256,128]{2,1,0:T(8,128)(2,1)S(1)}, u32[]{:S(2)}, u32[]{:S(2)}) collective-permute-start(bf16[4,256,128]{2,1,0:T(8,128)(2,1)S(1)} %all_to_all.5.refs_2_), channel_id=1, source_target_pairs={{0,64},{64,128},{128,192},{192,256},{256,320},{320,384},{384,448},... | collective-permute-start | bytes 786440 | tf_op jit(solution)/shard_map/ppermute | solution.py:254
  12.2 8.3 %collective-permute-start.5 = (bf16[4,256,128]{2,1,0:T(8,128)(2,1)S(1)}, bf16[4,256,128]{2,1,0:T(8,128)(2,1)S(1)}, u32[]{:S(2)}, u32[]{:S(2)}) collective-permute-start(bf16[4,256,128]{2,1,0:T(8,128)(2,1)S(1)} %all_to_all.5.refs_2_), channel_id=1, source_target_pairs={{0,448},{64,0},{128,64},{192,128},{256,192},{320,256},{384,320},{4... | collective-permute-start | bytes 786440 | tf_op jit(solution)/shard_map/ppermute | solution.py:255
  17.9 13.5 %collective-permute-start.2 = (bf16[4,256,128]{2,1,0:T(8,128)(2,1)S(1)}, bf16[4,256,128]{2,1,0:T(8,128)(2,1)S(1)}, u32[]{:S(2)}, u32[]{:S(2)}) collective-permute-start(bf16[4,256,128]{2,1,0:T(8,128)(2,1)S(1)} %collective-permute-done.1.refs_2_), channel_id=1, source_target_pairs={{0,64},{64,128},{128,192},{192,256},{256,320},{320,384},{384,448},... | collective-permute-start | bytes 786440 | tf_op jit(solution)/shard_map/ppermute | solution.py:254
  20.6 15.8 %collective-permute-start.6 = (bf16[4,256,128]{2,1,0:T(8,128)(2,1)S(1)}, bf16[4,256,128]{2,1,0:T(8,128)(2,1)S(1)}, u32[]{:S(2)}, u32[]{:S(2)}) collective-permute-start(bf16[4,256,128]{2,1,0:T(8,128)(2,1)S(1)} %collective-permute-done.5.refs_3_), channel_id=1, source_target_pairs={{0,448},{64,0},{128,64},{192,128},{256,192},{320,256},{384,320},{4... | collective-permute-start | bytes 786440 | tf_op jit(solution)/shard_map/ppermute | solution.py:255
  23.2 15.3 %copy-start.1 = (s32[16]{0:T(128)S(1)}, s32[16]{0:T(128)}, u32[]{:S(2)}) copy-start(s32[16]{0:T(128)} %refs_0_.9) | copy-start | bytes 196
  23.3 15.0 %collective-permute-start = (bf16[1024,128]{1,0:T(8,128)(2,1)S(1)}, bf16[1024,128]{1,0:T(8,128)(2,1)S(1)}, u32[]{:S(2)}, u32[]{:S(2)}) collective-permute-start(bf16[1024,128]{1,0:T(8,128)(2,1)S(1)} %bitcast.4), channel_id=1, source_target_pairs={{0,8},{8,0},{1,9},{9,1},{2,10},{10,2},{3,11},{11,3},{4,12},{12,4},... | collective-permute-start | bytes 786440 | tf_op jit(solution)/shard_map/ppermute | solution.py:244
  31.5 10.4 %collective-permute-start.3 = (bf16[4,256,128]{2,1,0:T(8,128)(2,1)S(1)}, bf16[4,256,128]{2,1,0:T(8,128)(2,1)S(1)}, u32[]{:S(2)}, u32[]{:S(2)}) collective-permute-start(bf16[4,256,128]{2,1,0:T(8,128)(2,1)S(1)} %collective-permute-done.2.refs_2_), channel_id=1, source_target_pairs={{0,64},{64,128},{128,192},{192,256},{256,320},{320,384},{384,448},... | collective-permute-start | bytes 786440 | tf_op jit(solution)/shard_map/ppermute | solution.py:254
  36.3 20.0 %collective-permute-start.7 = (bf16[4,256,128]{2,1,0:T(8,128)(2,1)S(1)}, bf16[4,256,128]{2,1,0:T(8,128)(2,1)S(1)}, u32[]{:S(2)}, u32[]{:S(2)}) collective-permute-start(bf16[4,256,128]{2,1,0:T(8,128)(2,1)S(1)} %collective-permute-done.6.refs_3_), channel_id=1, source_target_pairs={{0,448},{64,0},{128,64},{192,128},{256,192},{320,256},{384,320},{4... | collective-permute-start | bytes 786440 | tf_op jit(solution)/shard_map/ppermute | solution.py:255
  41.8 19.5 %collective-permute-start.4 = (bf16[4,256,128]{2,1,0:T(8,128)(2,1)S(1)}, bf16[4,256,128]{2,1,0:T(8,128)(2,1)S(1)}, u32[]{:S(2)}, u32[]{:S(2)}) collective-permute-start(bf16[4,256,128]{2,1,0:T(8,128)(2,1)S(1)} %collective-permute-done.3.refs_2_), channel_id=1, source_target_pairs={{0,64},{64,128},{128,192},{192,256},{256,320},{320,384},{384,448},... | collective-permute-start | bytes 786440 | tf_op jit(solution)/shard_map/ppermute | solution.py:259
  64.1 4.4 %collective-permute-start.8 = (bf16[144,1024]{1,0:T(8,128)(2,1)S(1)}, bf16[144,1024]{1,0:T(8,128)(2,1)S(1)}, u32[]{:S(2)}, u32[]{:S(2)}) collective-permute-start(bf16[144,1024]{1,0:T(8,128)(2,1)S(1)} %get-tuple-element.36), channel_id=1, source_target_pairs={{0,8},{8,0},{1,9},{9,1},{2,10},{10,2},{3,11},{11,3},{4,12},{12,4},... | collective-permute-start | bytes 884744 | tf_op jit(solution)/shard_map/ppermute | solution.py:261

commit v4 on v3

--- a/solution.py
+++ b/solution.py
@@ -11,7 +11,9 @@
 MASKED = -1.5e38
 START = -1.0e30
 FAR = 1 << 20
-COLUMNS = 1024
+COLUMNS = 512
+AHEAD = 1
+ROOM = 100.0
 VMEM_BYTES = 40 * 1024 * 1024
 VM = pl.BlockSpec(memory_space=pltpu.VMEM)
 SM = pl.BlockSpec(memory_space=pltpu.SMEM)
@@ -50,14 +52,6 @@
         m_out, l_out, a_out, p_out, m_ref, l_ref, a_ref, kv_ref, base = refs
     else:
         m_ref, l_ref, a_ref, kv_ref, base = refs
-    if first:
-        m_ref[...] = jnp.full(m_ref.shape, START, jnp.float32)
-        l_ref[...] = jnp.zeros(l_ref.shape, jnp.float32)
-        a_ref[...] = jnp.zeros(a_ref.shape, jnp.float32)
-    else:
-        m_ref[...] = m_in[...]
-        l_ref[...] = l_in[...]
-        a_ref[...] = a_in[...]
     depth, total = a_ref.shape
     mine = total // 2
     across, both_rows, _ = pieces[0].shape
@@ -73,13 +67,13 @@
     free = jnp.int32(0)
     for kind in (1, 2):
         for piece, shift in zip(pieces, shifts):
+            if kind == 2 and shift != 0:
+                continue
             row = lax.rem(blk + (down - shift), down)
             for column in range(across):
                 here = order[2 * row + column // per_span]
                 start = (column % per_span) * both_rows + core * rows
                 chosen = here < own_span if kind == 1 else here == own_span
-                if kind == 2 and shift != 0:
-                    continue
 
                 @pl.when(chosen)
                 def _():
@@ -87,70 +81,99 @@
                     base[free] = -FAR if kind == 1 else start
 
                 free = free + chosen.astype(jnp.int32)
-        if kind == 1:
-            visible = free
-
-    def fold(group, masked):
+    for i in range(count):
+
+        @pl.when(i >= free)
+        def _():
+            kv_ref[i] = jnp.zeros(kv_ref.shape[1:], kv_ref.dtype)
+
+    def hide(s, c, group):
+        if first:
+            shape = (rows, COLUMNS)
+            lane = lax.broadcasted_iota(jnp.int32, shape, 1) + c % mine
+            query_core = core if c < mine else 1 - core
+            gap = place + query_core * rows + lane // heads - lax.broadcasted_iota(jnp.int32, shape, 0)
+            seen = [gap >= base[i] for i in range(group)]
+        else:
+            seen = [i < free for i in range(group)]
+        return jnp.concatenate(
+            [jnp.where(seen[i], s[i * rows : (i + 1) * rows], MASKED) for i in range(group)], axis=0
+        )
+
+    def fold(group, partial, exact):
         blocks = [kv_ref[i] for i in range(group)]
         k = jnp.concatenate([b[:rows] for b in blocks], axis=0)
         v = jnp.concatenate([b[rows:] for b in blocks], axis=0)
         k = jnp.concatenate([k, k], axis=1)
-        parts = range(0, total, COLUMNS)
-        scores = [
-            jnp.dot(k, q_ref[:, c : c + COLUMNS], preferred_element_type=jnp.float32) for c in parts
-        ]
-        for c, s in zip(parts, scores):
+        parts = list(range(0, total, COLUMNS))
+        worst = jnp.zeros((1, COLUMNS), jnp.float32)
+
+        def score(c):
+            return jnp.dot(k, q_ref[:, c : c + COLUMNS], preferred_element_type=jnp.float32)
+
+        ahead = [score(c) for c in parts[:AHEAD]]
+        for i, c in enumerate(parts):
+            if i + AHEAD < len(parts):
+                ahead.append(score(parts[i + AHEAD]))
+            raw = ahead[i]
             at = pl.ds(c, COLUMNS)
-            if masked:
-                shape = (rows, COLUMNS)
-                lane = lax.broadcasted_iota(jnp.int32, shape, 1) + c % mine
-                query_core = core if c < mine else 1 - core
-                gap = place + query_core * rows + lane // heads - lax.broadcasted_iota(jnp.int32, shape, 0)
-                s = jnp.concatenate(
-                    [
-                        jnp.where(gap >= base[i], s[i * rows : (i + 1) * rows], MASKED)
-                        for i in range(group)
-                    ],
-                    axis=0,
-                )
-            m_old = m_ref[:, at]
-            m_new = jnp.maximum(m_old, jnp.max(s, axis=0, keepdims=True))
-            alpha = jnp.exp2(m_old - m_new)
-            p = jnp.exp2(s - m_new)
-            m_ref[:, at] = m_new
-            l_ref[:, at] = l_ref[:, at] * alpha + jnp.sum(p, axis=0, keepdims=True)
-            a_ref[:, at] = a_ref[:, at] * alpha + lax.dot_general(
+            s = hide(raw, c, group) if partial else raw
+            top = jnp.max(s, axis=0, keepdims=True)
+            if first:
+                m = jnp.where(top > 0.5 * MASKED, top, jnp.max(raw, axis=0, keepdims=True))
+            elif exact:
+                l_old = l_in[:, at]
+                m_old = jnp.where(l_old > 0.0, m_in[:, at], START)
+                m = jnp.maximum(m_old, top)
+                alpha = jnp.exp2(m_old - m)
+            else:
+                m = m_in[:, at]
+                low = (l_in[:, at] == 0.0) & (top > 0.5 * MASKED) & (top < m - ROOM)
+                worst = jnp.maximum(worst, jnp.where((top > m + ROOM) | low, 1.0, 0.0))
+            p = jnp.exp2(s - m)
+            l_new = jnp.sum(p, axis=0, keepdims=True)
+            a_new = lax.dot_general(
                 v,
                 p.astype(jnp.bfloat16),
                 (((0,), (0,)), ((), ())),
                 preferred_element_type=jnp.float32,
             )
-
-    @pl.when(visible == count)
-    def _():
-        fold(count, False)
-
-    if count > 4:
-
-        @pl.when((visible < count) & (free > 4))
+            m_ref[:, at] = m
+            if first:
+                l_ref[:, at] = l_new
+                a_ref[:, at] = a_new
+            elif exact:
+                l_ref[:, at] = l_old * alpha + l_new
+                a_ref[:, at] = a_in[:, at] * alpha + a_new
+            else:
+                l_ref[:, at] = l_in[:, at] + l_new
+                a_ref[:, at] = a_in[:, at] + a_new
+        return worst
+
+    if first:
+        fold(count, True, True)
+    else:
+        base[count] = 0
+
+        def attempt(group, partial):
+            base[count] = (jnp.max(fold(group, partial, False)) > 0.0).astype(jnp.int32)
+
+        @pl.when(free == 0)
         def _():
-            for i in range(4, count):
-
-                @pl.when(i >= free)
-                def _():
-                    kv_ref[i] = jnp.zeros(kv_ref.shape[1:], kv_ref.dtype)
-
-            fold(count, True)
-
-    @pl.when((visible < count) & (free > 0) & (free <= 4))
-    def _():
-        for i in range(1, 4):
-
-            @pl.when(i >= free)
-            def _():
-                kv_ref[i] = jnp.zeros(kv_ref.shape[1:], kv_ref.dtype)
-
-        fold(4, True)
+            m_ref[...] = m_in[...]
+            l_ref[...] = l_in[...]
+            a_ref[...] = a_in[...]
+
+        pl.when(free == count)(lambda: attempt(count, False))
+        if count > 4:
+            pl.when((free > 4) & (free < count))(lambda: attempt(count, True))
+            pl.when((free > 0) & (free <= 4))(lambda: attempt(4, True))
+        else:
+            pl.when((free > 0) & (free < count))(lambda: attempt(count, True))
+
+        @pl.when(base[count] > 0)
+        def _():
+            fold(count, True, True)
 
     if last:
         m_out[...] = m_ref[:, :mine]
@@ -253,6 +276,8 @@
     for hop in range(1, down // 2):
         rising = lax.ppermute(rising, "blk", up)
         falling = lax.ppermute(falling, "blk", back)
+        if hop <= 2:
+            rising, state = lax.optimization_barrier((rising, state))
         state = attend(
             span_order, q, [rising, falling], [hop, down - hop], state, False, heads, down
         )

time: 69.8 us -> 64.4 us (0.923)
  the two profiles are of different devices: /device:TPU:57 before, /device:TPU:1 now
where the time goes in v4:
time: 64.4 us; the launch traced here: 64 us
  starting transfers between devices  43.7 us (68%)
  Pallas kernels  12.9 us (20%)
  waiting for transfers between devices  5.64 us (9%)
  other arithmetic  0.78 us (1%)
  local copies, waits for them, and re-layouts  0.74 us (1%)
    ppermute x3, starting transfers between devices, local(): falling = lax.ppermute(falling, 'blk', back)  13.7 us
    pallas_call x5, Pallas kernels, attend(): pl.pallas_call(body, out_shape=out_shape, in_specs=[SM] + [VM] * (len(arg...  11.7 us
    ppermute x1, starting transfers between devices, local(): packet = lax.ppermute(packet, 'core', swap)  9.95 us
    ppermute x4, starting transfers between devices, local(): rising = lax.ppermute(rising, 'blk', up)  7.67 us
    ppermute x1, starting transfers between devices, local(): other = lax.ppermute(own, 'core', swap)  7.38 us
    all_to_all x1, starting transfers between devices, local(): row = lax.all_to_all(copies, 'x', 0, 0, tiled=True)  4.97 us
    ppermute x4, waiting for transfers between devices, local(): rising = lax.ppermute(rising, 'blk', up)  4.44 us
  transfers between devices with their start and end apart: 10, of which 3 were waited for; matrix products, arithmetic and copies ran while one was open for 0% of the time, Pallas kernels for 16%

profile of v4, /device:TPU:1, one launch (start us, length us, event | category | flops | bytes accessed | tf_op | source)
XLA Modules:
  0.0 64.0 jit_solution(1315144174424412162)
XLA Ops:
  0.0 0.8 %pad_maximum_fusion = bf16[256,128]{1,0:T(8,128)(2,1)S(1)} fusion(bf16[128,128]{1,0:T(8,128)(2,1)} %bitcast.6, bf16[128,128]{1,0:T(8,128)(2,1)} %bitcast.7), kind=kLoop, calls=%fused_computation | loop fusion | flops 131072 | bytes 131072 | tf_op jit(solution)/shard_map/concatenate | solution.py:268
  0.8 0.7 %broadcast_in_dim.2 = bf16[4,256,128]{2,1,0:T(8,128)(2,1)} broadcast(bf16[256,128]{1,0:T(8,128)(2,1)S(1)} %pad_maximum_fusion), dimensions={1,2} | broadcast | bytes 327680 | tf_op jit(solution)/shard_map/broadcast_in_dim | solution.py:269
  1.5 5.0 %all-to-all-start = ((bf16[4,256,128]{2,1,0:T(8,128)(2,1)}), bf16[4,256,128]{2,1,0:T(8,128)(2,1)S(1)}, u32[]{:S(2)}, u32[]{:S(2)}) async-start(bf16[4,256,128]{2,1,0:T(8,128)(2,1)} %broadcast_in_dim.2), calls=%async_computation | async-start | bytes 524288 | tf_op jit(solution)/shard_map/all_to_all | solution.py:270
  6.5 7.4 %collective-permute-start = (bf16[1024,128]{1,0:T(8,128)(2,1)S(1)}, bf16[1024,128]{1,0:T(8,128)(2,1)S(1)}, u32[]{:S(2)}, u32[]{:S(2)}) collective-permute-start(bf16[1024,128]{1,0:T(8,128)(2,1)S(1)} %bitcast.4), channel_id=1, source_target_pairs={{0,8},{8,0},{1,9},{9,1},{2,10},{10,2},{3,11},{11,3},{4,12},{12,4},... | collective-permute-start | bytes 786440 | tf_op jit(solution)/shard_map/ppermute | solution.py:267
  13.9 1.9 %collective-permute-start.1 = (bf16[4,256,128]{2,1,0:T(8,128)(2,1)S(1)}, bf16[4,256,128]{2,1,0:T(8,128)(2,1)S(1)}, u32[]{:S(2)}, u32[]{:S(2)}) collective-permute-start(bf16[4,256,128]{2,1,0:T(8,128)(2,1)S(1)} %all-to-all-done.refs_2_), channel_id=1, source_target_pairs={{0,64},{64,128},{128,192},{192,256},{256,320},{320,384},{384,448},... | collective-permute-start | bytes 786440 | tf_op jit(solution)/shard_map/ppermute | solution.py:277
  15.8 4.6 %collective-permute-start.3 = (bf16[4,256,128]{2,1,0:T(8,128)(2,1)S(1)}, bf16[4,256,128]{2,1,0:T(8,128)(2,1)S(1)}, u32[]{:S(2)}, u32[]{:S(2)}) collective-permute-start(bf16[4,256,128]{2,1,0:T(8,128)(2,1)S(1)} %all-to-all-done.refs_2_), channel_id=1, source_target_pairs={{0,448},{64,0},{128,64},{192,128},{256,192},{320,256},{384,320},{4... | collective-permute-start | bytes 786440 | tf_op jit(solution)/shard_map/ppermute | solution.py:278
  20.4 0.0 collective-permute-done.other_ref
  20.4 0.3 shard_map.46.refs_1_
  20.7 2.4 %shard_map.47 = (f32[1,2048]{1,0:T(1,128)S(1)}, f32[1,2048]{1,0:T(1,128)S(1)}, f32[128,2048]{1,0:T(8,128)S(1)}) custom-call(s32[16]{0:T(128)S(1)} %copy-done.1, bf16[256,2048]{1,0:T(8,128)(2,1)S(1)} %shard_map.46.refs_1_, bf16[4,256,128]{2,1,0:T(8,128)(2,1)S(1)} %all-to-all-done.refs_2_), custom_call_target="tpu_custom_call" | custom-call | flops 536870912 | bytes 786432 | tf_op jit(solution)/shard_map/pallas_call | solution.py:223
  23.1 0.0 collective-permute-done.1.refs_2_
  23.1 1.9 %collective-permute-start.2 = (bf16[4,256,128]{2,1,0:T(8,128)(2,1)S(1)}, bf16[4,256,128]{2,1,0:T(8,128)(2,1)S(1)}, u32[]{:S(2)}, u32[]{:S(2)}) collective-permute-start(bf16[4,256,128]{2,1,0:T(8,128)(2,1)S(1)} %collective-permute-done.1.refs_2_), channel_id=1, source_target_pairs={{0,64},{64,128},{128,192},{192,256},{256,320},{320,384},{384,448},... | collective-permute-start | bytes 786440 | tf_op jit(solution)/shard_map/ppermute | solution.py:277
  25.1 4.6 %collective-permute-start.6 = (bf16[4,256,128]{2,1,0:T(8,128)(2,1)S(1)}, bf16[4,256,128]{2,1,0:T(8,128)(2,1)S(1)}, u32[]{:S(2)}, u32[]{:S(2)}) collective-permute-start(bf16[4,256,128]{2,1,0:T(8,128)(2,1)S(1)} %collective-permute-done.3.refs_3_), channel_id=1, source_target_pairs={{0,448},{64,0},{128,64},{192,128},{256,192},{320,256},{384,320},{4... | collective-permute-start | bytes 786440 | tf_op jit(solution)/shard_map/ppermute | solution.py:278
  29.6 2.8 %shard_map.48 = (f32[1,2048]{1,0:T(1,128)S(1)}, f32[1,2048]{1,0:T(1,128)S(1)}, f32[128,2048]{1,0:T(8,128)S(1)}) custom-call(s32[16]{0:T(128)S(1)} %copy-done.1, bf16[256,2048]{1,0:T(8,128)(2,1)S(1)} %shard_map.46.refs_1_, bf16[4,256,128]{2,1,0:T(8,128)(2,1)S(1)} %collective-permute-done.1.refs_2_, bf16[4,256,128]{2,1,0:T(8,128)(2,1)S(1)} %collective-permute-done.3.refs_3_, ...), custom_call_target="tpu_custom_call" | custom-call | flops 1073741824 | bytes 1048576 | tf_op jit(solution)/shard_map/pallas_call | solution.py:223
  32.4 1.9 %collective-permute-start.4 = (bf16[4,256,128]{2,1,0:T(8,128)(2,1)S(1)}, bf16[4,256,128]{2,1,0:T(8,128)(2,1)S(1)}, u32[]{:S(2)}, u32[]{:S(2)}) collective-permute-start(bf16[4,256,128]{2,1,0:T(8,128)(2,1)S(1)} %collective-permute-done.2.refs_2_), channel_id=1, source_target_pairs={{0,64},{64,128},{128,192},{192,256},{256,320},{320,384},{384,448},... | collective-permute-start | bytes 786440 | tf_op jit(solution)/shard_map/ppermute | solution.py:277
  34.4 4.6 %collective-permute-start.7 = (bf16[4,256,128]{2,1,0:T(8,128)(2,1)S(1)}, bf16[4,256,128]{2,1,0:T(8,128)(2,1)S(1)}, u32[]{:S(2)}, u32[]{:S(2)}) collective-permute-start(bf16[4,256,128]{2,1,0:T(8,128)(2,1)S(1)} %collective-permute-done.6.refs_3_), channel_id=1, source_target_pairs={{0,448},{64,0},{128,64},{192,128},{256,192},{320,256},{384,320},{4... | collective-permute-start | bytes 786440 | tf_op jit(solution)/shard_map/ppermute | solution.py:278
  39.0 1.8 %collective-permute-done.4.refs_2_ = bf16[4,256,128]{2,1,0:T(8,128)(2,1)S(1)} collective-permute-done((bf16[4,256,128]{2,1,0:T(8,128)(2,1)S(1)}, bf16[4,256,128]{2,1,0:T(8,128)(2,1)S(1)}, u32[]{:S(2)}, u32[]{:S(2)}) %collective-permute-start.4) | collective-permute-done | bytes 262176 | tf_op jit(solution)/shard_map/ppermute | solution.py:277
  40.8 1.9 %collective-permute-start.5 = (bf16[4,256,128]{2,1,0:T(8,128)(2,1)S(1)}, bf16[4,256,128]{2,1,0:T(8,128)(2,1)S(1)}, u32[]{:S(2)}, u32[]{:S(2)}) collective-permute-start(bf16[4,256,128]{2,1,0:T(8,128)(2,1)S(1)} %collective-permute-done.4.refs_2_), channel_id=1, source_target_pairs={{0,64},{64,128},{128,192},{192,256},{256,320},{320,384},{384,448},... | collective-permute-start | bytes 786440 | tf_op jit(solution)/shard_map/ppermute | solution.py:284
  42.7 2.2 %shard_map.49 = (f32[1,2048]{1,0:T(1,128)S(1)}, f32[1,2048]{1,0:T(1,128)S(1)}, f32[128,2048]{1,0:T(8,128)S(1)}) custom-call(s32[16]{0:T(128)S(1)} %copy-done.1, bf16[256,2048]{1,0:T(8,128)(2,1)S(1)} %shard_map.46.refs_1_, bf16[4,256,128]{2,1,0:T(8,128)(2,1)S(1)} %collective-permute-done.2.refs_2_, bf16[4,256,128]{2,1,0:T(8,128)(2,1)S(1)} %collective-permute-done.6.refs_3_, ...), custom_call_target="tpu_custom_call" | custom-call | flops 1073741824 | bytes 1048576 | tf_op jit(solution)/shard_map/pallas_call | solution.py:223
  44.9 2.3 %shard_map.50 = (f32[1,2048]{1,0:T(1,128)S(1)}, f32[1,2048]{1,0:T(1,128)S(1)}, f32[128,2048]{1,0:T(8,128)S(1)}) custom-call(s32[16]{0:T(128)S(1)} %copy-done.1, bf16[256,2048]{1,0:T(8,128)(2,1)S(1)} %shard_map.46.refs_1_, bf16[4,256,128]{2,1,0:T(8,128)(2,1)S(1)} %collective-permute-done.4.refs_2_, bf16[4,256,128]{2,1,0:T(8,128)(2,1)S(1)} %collective-permute-done.7.refs_3_, ...), custom_call_target="tpu_custom_call" | custom-call | flops 1073741824 | bytes 1048576 | tf_op jit(solution)/shard_map/pallas_call | solution.py:223
  47.2 2.6 %collective-permute-done.5.refs_2_ = bf16[4,256,128]{2,1,0:T(8,128)(2,1)S(1)} collective-permute-done((bf16[4,256,128]{2,1,0:T(8,128)(2,1)S(1)}, bf16[4,256,128]{2,1,0:T(8,128)(2,1)S(1)}, u32[]{:S(2)}, u32[]{:S(2)}) %collective-permute-start.5) | collective-permute-done | bytes 262176 | tf_op jit(solution)/shard_map/ppermute | solution.py:284
  49.8 2.1 %shard_map.51 = (f32[1,1024]{1,0:T(1,128)S(1)}, f32[1,1024]{1,0:T(1,128)S(1)}, f32[128,1024]{1,0:T(8,128)S(1)}, bf16[144,1024]{1,0:T(8,128)(2,1)S(1)}) custom-call(s32[16]{0:T(128)S(1)} %copy-done.1, bf16[256,2048]{1,0:T(8,128)(2,1)S(1)} %shard_map.46.refs_1_, bf16[4,256,128]{2,1,0:T(8,128)(2,1)S(1)} %collective-permute-done.5.refs_2_, ...), custom_call_target="tpu_custom_call" | custom-call | flops 536870912 | bytes 786432 | tf_op jit(solution)/shard_map/pallas_call | solution.py:223
  51.9 10.0 %collective-permute-start.8 = (bf16[144,1024]{1,0:T(8,128)(2,1)S(1)}, bf16[144,1024]{1,0:T(8,128)(2,1)S(1)}, u32[]{:S(2)}, u32[]{:S(2)}) collective-permute-start(bf16[144,1024]{1,0:T(8,128)(2,1)S(1)} %get-tuple-element.52), channel_id=1, source_target_pairs={{0,8},{8,0},{1,9},{9,1},{2,10},{10,2},{3,11},{11,3},{4,12},{12,4},... | collective-permute-start | bytes 884744 | tf_op jit(solution)/shard_map/ppermute | solution.py:286
  61.9 1.2 %collective-permute-done.8.p_ref = bf16[144,1024]{1,0:T(8,128)(2,1)S(1)} collective-permute-done((bf16[144,1024]{1,0:T(8,128)(2,1)S(1)}, bf16[144,1024]{1,0:T(8,128)(2,1)S(1)}, u32[]{:S(2)}, u32[]{:S(2)}) %collective-permute-start.8) | collective-permute-done | bytes 294944 | tf_op jit(solution)/shard_map/ppermute | solution.py:286
  63.1 0.9 %shard_map.52 = bf16[1024,128]{1,0:T(8,128)(2,1)} custom-call(f32[1,1024]{1,0:T(1,128)S(1)} %get-tuple-element.49.m_ref, f32[1,1024]{1,0:T(1,128)S(1)} %get-tuple-element.50.l_ref, f32[128,1024]{1,0:T(8,128)S(1)} %get-tuple-element.51.a_ref, bf16[144,1024]{1,0:T(8,128)(2,1)S(1)} %collective-permute-done.8.p_ref), custom_call_target="tpu_custom_call" | custom-call | tf_op jit(solution)/shard_map/pallas_call | solution.py:253
  (9 shorter events, 0.0 us)
Async XLA Ops:
  1.5 5.0 %copy-start = (bf16[128,8,128]{2,1,0:T(8,128)(2,1)S(1)}, bf16[128,8,128]{2,1,0:T(8,128)(2,1)}, u32[]{:S(2)}) copy-start(bf16[128,8,128]{2,1,0:T(8,128)(2,1)} %param.4) | copy-start | bytes 786436
  1.5 12.4 %all-to-all-start = ((bf16[4,256,128]{2,1,0:T(8,128)(2,1)}), bf16[4,256,128]{2,1,0:T(8,128)(2,1)S(1)}, u32[]{:S(2)}, u32[]{:S(2)}) async-start(bf16[4,256,128]{2,1,0:T(8,128)(2,1)} %broadcast_in_dim.2), calls=%async_computation | async-start | bytes 524288 | tf_op jit(solution)/shard_map/all_to_all | solution.py:270
  6.5 14.2 %copy-start.1 = (s32[16]{0:T(128)S(1)}, s32[16]{0:T(128)}, u32[]{:S(2)}) copy-start(s32[16]{0:T(128)} %refs_0_.9) | copy-start | bytes 196
  6.5 13.9 %collective-permute-start = (bf16[1024,128]{1,0:T(8,128)(2,1)S(1)}, bf16[1024,128]{1,0:T(8,128)(2,1)S(1)}, u32[]{:S(2)}, u32[]{:S(2)}) collective-permute-start(bf16[1024,128]{1,0:T(8,128)(2,1)S(1)} %bitcast.4), channel_id=1, source_target_pairs={{0,8},{8,0},{1,9},{9,1},{2,10},{10,2},{3,11},{11,3},{4,12},{12,4},... | collective-permute-start | bytes 786440 | tf_op jit(solution)/shard_map/ppermute | solution.py:267
  13.9 9.2 %collective-permute-start.1 = (bf16[4,256,128]{2,1,0:T(8,128)(2,1)S(1)}, bf16[4,256,128]{2,1,0:T(8,128)(2,1)S(1)}, u32[]{:S(2)}, u32[]{:S(2)}) collective-permute-start(bf16[4,256,128]{2,1,0:T(8,128)(2,1)S(1)} %all-to-all-done.refs_2_), channel_id=1, source_target_pairs={{0,64},{64,128},{128,192},{192,256},{256,320},{320,384},{384,448},... | collective-permute-start | bytes 786440 | tf_op jit(solution)/shard_map/ppermute | solution.py:277
  15.8 9.2 %collective-permute-start.3 = (bf16[4,256,128]{2,1,0:T(8,128)(2,1)S(1)}, bf16[4,256,128]{2,1,0:T(8,128)(2,1)S(1)}, u32[]{:S(2)}, u32[]{:S(2)}) collective-permute-start(bf16[4,256,128]{2,1,0:T(8,128)(2,1)S(1)} %all-to-all-done.refs_2_), channel_id=1, source_target_pairs={{0,448},{64,0},{128,64},{192,128},{256,192},{320,256},{384,320},{4... | collective-permute-start | bytes 786440 | tf_op jit(solution)/shard_map/ppermute | solution.py:278
  23.1 9.3 %collective-permute-start.2 = (bf16[4,256,128]{2,1,0:T(8,128)(2,1)S(1)}, bf16[4,256,128]{2,1,0:T(8,128)(2,1)S(1)}, u32[]{:S(2)}, u32[]{:S(2)}) collective-permute-start(bf16[4,256,128]{2,1,0:T(8,128)(2,1)S(1)} %collective-permute-done.1.refs_2_), channel_id=1, source_target_pairs={{0,64},{64,128},{128,192},{192,256},{256,320},{320,384},{384,448},... | collective-permute-start | bytes 786440 | tf_op jit(solution)/shard_map/ppermute | solution.py:277
  25.1 9.3 %collective-permute-start.6 = (bf16[4,256,128]{2,1,0:T(8,128)(2,1)S(1)}, bf16[4,256,128]{2,1,0:T(8,128)(2,1)S(1)}, u32[]{:S(2)}, u32[]{:S(2)}) collective-permute-start(bf16[4,256,128]{2,1,0:T(8,128)(2,1)S(1)} %collective-permute-done.3.refs_3_), channel_id=1, source_target_pairs={{0,448},{64,0},{128,64},{192,128},{256,192},{320,256},{384,320},{4... | collective-permute-start | bytes 786440 | tf_op jit(solution)/shard_map/ppermute | solution.py:278
  32.4 8.3 %collective-permute-start.4 = (bf16[4,256,128]{2,1,0:T(8,128)(2,1)S(1)}, bf16[4,256,128]{2,1,0:T(8,128)(2,1)S(1)}, u32[]{:S(2)}, u32[]{:S(2)}) collective-permute-start(bf16[4,256,128]{2,1,0:T(8,128)(2,1)S(1)} %collective-permute-done.2.refs_2_), channel_id=1, source_target_pairs={{0,64},{64,128},{128,192},{192,256},{256,320},{320,384},{384,448},... | collective-permute-start | bytes 786440 | tf_op jit(solution)/shard_map/ppermute | solution.py:277
  34.4 10.6 %collective-permute-start.7 = (bf16[4,256,128]{2,1,0:T(8,128)(2,1)S(1)}, bf16[4,256,128]{2,1,0:T(8,128)(2,1)S(1)}, u32[]{:S(2)}, u32[]{:S(2)}) collective-permute-start(bf16[4,256,128]{2,1,0:T(8,128)(2,1)S(1)} %collective-permute-done.6.refs_3_), channel_id=1, source_target_pairs={{0,448},{64,0},{128,64},{192,128},{256,192},{320,256},{384,320},{4... | collective-permute-start | bytes 786440 | tf_op jit(solution)/shard_map/ppermute | solution.py:278
  40.8 9.1 %collective-permute-start.5 = (bf16[4,256,128]{2,1,0:T(8,128)(2,1)S(1)}, bf16[4,256,128]{2,1,0:T(8,128)(2,1)S(1)}, u32[]{:S(2)}, u32[]{:S(2)}) collective-permute-start(bf16[4,256,128]{2,1,0:T(8,128)(2,1)S(1)} %collective-permute-done.4.refs_2_), channel_id=1, source_target_pairs={{0,64},{64,128},{128,192},{192,256},{256,320},{320,384},{384,448},... | collective-permute-start | bytes 786440 | tf_op jit(solution)/shard_map/ppermute | solution.py:284
  51.9 11.1 %collective-permute-start.8 = (bf16[144,1024]{1,0:T(8,128)(2,1)S(1)}, bf16[144,1024]{1,0:T(8,128)(2,1)S(1)}, u32[]{:S(2)}, u32[]{:S(2)}) collective-permute-start(bf16[144,1024]{1,0:T(8,128)(2,1)S(1)} %get-tuple-element.52), channel_id=1, source_target_pairs={{0,8},{8,0},{1,9},{9,1},{2,10},{10,2},{3,11},{11,3},{4,12},{12,4},... | collective-permute-start | bytes 884744 | tf_op jit(solution)/shard_map/ppermute | solution.py:286

commit v5 on v4

--- a/solution.py
+++ b/solution.py
@@ -44,15 +44,16 @@
     )(q, other)
 
 
-def attend_kernel(shifts, down, first, last, heads, order, q_ref, *refs):
+def attend_kernel(shifts, down, columns, state_in, theirs, heads, order, q_ref, *refs):
     pieces, refs = refs[: len(shifts)], refs[len(shifts) :]
+    first = not state_in
     if not first:
         m_in, l_in, a_in, *refs = refs
-    if last:
-        m_out, l_out, a_out, p_out, m_ref, l_ref, a_ref, kv_ref, base = refs
-    else:
-        m_ref, l_ref, a_ref, kv_ref, base = refs
-    depth, total = a_ref.shape
+    if theirs:
+        p_out, *refs = refs
+    m_ref, l_ref, a_ref, kv_ref, base = refs
+    low_column, high_column = columns
+    depth, total = a_ref.shape[0], q_ref.shape[1]
     mine = total // 2
     across, both_rows, _ = pieces[0].shape
     rows = both_rows // 2
@@ -105,7 +106,7 @@
         k = jnp.concatenate([b[:rows] for b in blocks], axis=0)
         v = jnp.concatenate([b[rows:] for b in blocks], axis=0)
         k = jnp.concatenate([k, k], axis=1)
-        parts = list(range(0, total, COLUMNS))
+        parts = list(range(low_column, high_column, COLUMNS))
         worst = jnp.zeros((1, COLUMNS), jnp.float32)
 
         def score(c):
@@ -116,7 +117,7 @@
             if i + AHEAD < len(parts):
                 ahead.append(score(parts[i + AHEAD]))
             raw = ahead[i]
-            at = pl.ds(c, COLUMNS)
+            at, to = pl.ds(c, COLUMNS), pl.ds(c - low_column, COLUMNS)
             s = hide(raw, c, group) if partial else raw
             top = jnp.max(s, axis=0, keepdims=True)
             if first:
@@ -138,16 +139,16 @@
                 (((0,), (0,)), ((), ())),
                 preferred_element_type=jnp.float32,
             )
-            m_ref[:, at] = m
+            m_ref[:, to] = m
             if first:
-                l_ref[:, at] = l_new
-                a_ref[:, at] = a_new
+                l_ref[:, to] = l_new
+                a_ref[:, to] = a_new
             elif exact:
-                l_ref[:, at] = l_old * alpha + l_new
-                a_ref[:, at] = a_in[:, at] * alpha + a_new
+                l_ref[:, to] = l_old * alpha + l_new
+                a_ref[:, to] = a_in[:, at] * alpha + a_new
             else:
-                l_ref[:, at] = l_in[:, at] + l_new
-                a_ref[:, at] = a_in[:, at] + a_new
+                l_ref[:, to] = l_in[:, at] + l_new
+                a_ref[:, to] = a_in[:, at] + a_new
         return worst
 
     if first:
@@ -160,9 +161,9 @@
 
         @pl.when(free == 0)
         def _():
-            m_ref[...] = m_in[...]
-            l_ref[...] = l_in[...]
-            a_ref[...] = a_in[...]
+            m_ref[...] = m_in[:, low_column:high_column]
+            l_ref[...] = l_in[:, low_column:high_column]
+            a_ref[...] = a_in[:, low_column:high_column]
 
         pl.when(free == count)(lambda: attempt(count, False))
         if count > 4:
@@ -175,14 +176,11 @@
         def _():
             fold(count, True, True)
 
-    if last:
-        m_out[...] = m_ref[:, :mine]
-        l_out[...] = l_ref[:, :mine]
-        a_out[...] = a_ref[:, :mine]
-        l = l_ref[:, mine:]
+    if theirs:
+        l = l_ref[...]
         some = l > 0.0
-        p_out[:depth, :] = (a_ref[:, mine:] / jnp.where(some, l, 1.0)).astype(jnp.bfloat16)
-        level = jnp.where(some, m_ref[:, mine:] + jnp.log(jnp.where(some, l, 1.0)) * LOG2E, START)
+        p_out[:depth, :] = (a_ref[...] / jnp.where(some, l, 1.0)).astype(jnp.bfloat16)
+        level = jnp.where(some, m_ref[...] + jnp.log(jnp.where(some, l, 1.0)) * LOG2E, START)
         high, rest = split(level)
         mid, rest = split(rest)
         line = lax.broadcasted_iota(jnp.int32, (p_out.shape[0] - depth, mine), 0)
@@ -194,30 +192,25 @@
         p_out[depth:, :] = packed.astype(jnp.bfloat16)
 
 
-def attend(order, q, pieces, shifts, state, last, heads, down):
+def attend(order, q, pieces, shifts, state, heads, down, columns=None, theirs=False):
     total = q.shape[1]
+    columns = columns or (0, total)
+    width = columns[1] - columns[0]
     across, both_rows, head_size = pieces[0].shape
     count = across * len(pieces)
-    first = state is None
-    args = [order, q] + list(pieces) + ([] if first else list(state))
-
-    def shapes(n):
-        stat = jax.ShapeDtypeStruct((1, n), jnp.float32)
-        return [stat, stat, jax.ShapeDtypeStruct((head_size, n), jnp.float32)]
-
-    extra = [
+    args = [order, q] + list(pieces) + list(state)
+    stat = jax.ShapeDtypeStruct((1, width), jnp.float32)
+    out_shape = [stat, stat, jax.ShapeDtypeStruct((head_size, width), jnp.float32)]
+    scratch = [
         pltpu.VMEM((count, both_rows, head_size), jnp.bfloat16),
         pltpu.SMEM((count + 1,), jnp.int32),
     ]
-    if last:
-        packet = jax.ShapeDtypeStruct((head_size + 16, total // 2), jnp.bfloat16)
-        out_shape = shapes(total // 2) + [packet]
-        scratch = [pltpu.VMEM(s.shape, s.dtype) for s in shapes(total)] + extra
-    else:
-        out_shape, scratch = shapes(total), extra
+    if theirs:
+        scratch = [pltpu.VMEM(s.shape, s.dtype) for s in out_shape] + scratch
+        out_shape = [jax.ShapeDtypeStruct((head_size + 16, width), jnp.bfloat16)]
 
     def body(*refs):
-        attend_kernel(shifts, down, first, last, heads, *refs)
+        attend_kernel(shifts, down, columns, len(state) > 0, theirs, heads, *refs)
 
     keys = count * both_rows // 2
     return pl.pallas_call(
@@ -228,9 +221,9 @@
         scratch_shapes=scratch,
         compiler_params=PARAMS,
         cost_estimate=pl.CostEstimate(
-            flops=4 * total * keys * head_size,
-            bytes_accessed=4 * keys * head_size + 2 * total * head_size,
-            transcendentals=total * keys,
+            flops=4 * width * keys * head_size,
+            bytes_accessed=4 * keys * head_size + 2 * width * head_size,
+            transcendentals=width * keys,
         ),
     )(*args)
 
@@ -265,26 +258,32 @@
     swap = [(0, 1), (1, 0)]
     own = queries.reshape(rows * heads, head_size)
     other = lax.ppermute(own, "core", swap)
-    kv = jnp.concatenate([keys.reshape(rows, head_size), values.reshape(rows, head_size)], axis=0)
-    copies = jnp.broadcast_to(kv[None], (across, 2 * rows, head_size))
-    row = lax.all_to_all(copies, "x", 0, 0, tiled=True)
+    wide = (across, rows, head_size)
+    k = jnp.broadcast_to(keys.reshape(1, rows, head_size), wide)
+    v = jnp.broadcast_to(values.reshape(1, rows, head_size), wide)
+    spread = jnp.concatenate([k, v], axis=1)
+    row = lax.all_to_all(spread, "x", 0, 0, tiled=True)
     up = [(i, (i + 1) % down) for i in range(down)]
     back = [(i, (i - 1) % down) for i in range(down)]
     q = prepare(own, other)
-    state = attend(span_order, q, [row], [0], None, False, heads, down)
+    state = attend(span_order, q, [row], [0], (), heads, down)
     rising = falling = row
     for hop in range(1, down // 2):
         rising = lax.ppermute(rising, "blk", up)
         falling = lax.ppermute(falling, "blk", back)
         if hop <= 2:
             rising, state = lax.optimization_barrier((rising, state))
-        state = attend(
-            span_order, q, [rising, falling], [hop, down - hop], state, False, heads, down
-        )
-    rising = lax.ppermute(rising, "blk", up)
-    m, l, a, packet = attend(span_order, q, [rising], [down // 2], state, True, heads, down)
-    packet = lax.ppermute(packet, "core", swap)
-    return combine(m, l, a, packet).reshape(rows, heads, head_size)
+        state = attend(span_order, q, [rising, falling], [hop, down - hop], state, heads, down)
+    farthest = lax.ppermute(rising, "blk", up)
+    mine = q.shape[1] // 2
+    half, other_half = (0, mine), (mine, 2 * mine)
+    (packet,) = attend(
+        span_order, q, [farthest], [down // 2], state, heads, down, other_half, True
+    )
+    packet, state = lax.optimization_barrier((packet, state))
+    theirs = lax.ppermute(packet, "core", swap)
+    m, l, a = attend(span_order, q, [farthest], [down // 2], state, heads, down, half)
+    return combine(m, l, a, theirs).reshape(rows, heads, head_size)
 
 
 def solution(mesh):

time: 64.4 us -> 63.7 us (0.989)
  Pallas kernels: 12.9 us -> 7.84 us
  waiting for transfers between devices: 5.64 us -> 9.14 us
    pallas_call x5 -> x6, Pallas kernels: 11.7 us -> 6.67 us  [attend(): pl.pallas_call(body, out_shape=out_shape, in_specs=[SM] + [VM] * (len(arg...]
    ppermute x1 -> x2, waiting for transfers between devices: 1.19 us -> 6.13 us  [the longest x1 5.64 us: local(): farthest = lax.ppermute(rising, 'blk', up)]
    ppermute x1 -> x2, starting transfers between devices: 9.95 us -> 12.4 us  [the longest x1 10.5 us: local(): theirs = lax.ppermute(packet, 'core', swap)]
    ppermute x4 -> x3, starting transfers between devices: 7.67 us -> 5.75 us  [local(): rising = lax.ppermute(rising, 'blk', up)]
    ppermute x4 -> x3, waiting for transfers between devices: 4.44 us -> 3 us  [local(): rising = lax.ppermute(rising, 'blk', up)]
  transfers between devices with their start and end apart: 10 -> 10, of which waited for: 3 -> 4; matrix products, arithmetic and copies ran while one was open for 0% -> 0% of each run, Pallas kernels for 16% -> 10%
where the time goes in v5:
time: 63.7 us; the launch traced here: 62.9 us
  starting transfers between devices  44.2 us (69%)
  waiting for transfers between devices  9.14 us (14%)
  Pallas kernels  7.84 us (12%)
  local copies, waits for them, and re-layouts  0.81 us (1%)
  other arithmetic  0.72 us (1%)
    ppermute x3, starting transfers between devices, local(): falling = lax.ppermute(falling, 'blk', back)  13.7 us
    ppermute x1, starting transfers between devices, local(): theirs = lax.ppermute(packet, 'core', swap)  10.5 us
    ppermute x1, starting transfers between devices, local(): other = lax.ppermute(own, 'core', swap)  7.38 us
    pallas_call x6, Pallas kernels, attend(): pl.pallas_call(body, out_shape=out_shape, in_specs=[SM] + [VM] * (len(arg...  6.67 us
    ppermute x3, starting transfers between devices, local(): rising = lax.ppermute(rising, 'blk', up)  5.75 us
    ppermute x1, waiting for transfers between devices, local(): farthest = lax.ppermute(rising, 'blk', up)  5.64 us
    all_to_all x1, starting transfers between devices, local(): row = lax.all_to_all(spread, 'x', 0, 0, tiled=True)  4.97 us
    ppermute x3, waiting for transfers between devices, local(): rising = lax.ppermute(rising, 'blk', up)  3 us
  transfers between devices with their start and end apart: 10, of which 4 were waited for; matrix products, arithmetic and copies ran while one was open for 0% of the time, Pallas kernels for 10%

profile of v5, /device:TPU:1, one launch (start us, length us, event | category | flops | bytes accessed | tf_op | source)
XLA Modules:
  0.0 62.9 jit_solution(1656284126703583731)
XLA Ops:
  0.0 0.8 %broadcast_in_dim.15 = bf16[4,128,128]{2,1,0:T(8,128)(2,1)S(1)} broadcast(bf16[128,128]{1,0:T(8,128)(2,1)} %bitcast.6), dimensions={1,2} | broadcast | bytes 163840 | tf_op jit(solution)/shard_map/broadcast_in_dim | solution.py:262
  0.8 0.7 %pad_maximum_fusion = bf16[4,256,128]{2,1,0:T(8,128)(2,1)} fusion(bf16[4,128,128]{2,1,0:T(8,128)(2,1)S(1)} %broadcast_in_dim.17, bf16[4,128,128]{2,1,0:T(8,128)(2,1)S(1)} %broadcast_in_dim.15), kind=kLoop, calls=%fused_computation | loop fusion | flops 524288 | bytes 524288 | tf_op jit(solution)/shard_map/concatenate | solution.py:264
  1.5 5.0 %all-to-all-start = ((bf16[4,256,128]{2,1,0:T(8,128)(2,1)}), bf16[4,256,128]{2,1,0:T(8,128)(2,1)S(1)}, u32[]{:S(2)}, u32[]{:S(2)}) async-start(bf16[4,256,128]{2,1,0:T(8,128)(2,1)} %pad_maximum_fusion), calls=%async_computation | async-start | bytes 524288 | tf_op jit(solution)/shard_map/all_to_all | solution.py:265
  6.5 7.4 %collective-permute-start = (bf16[1024,128]{1,0:T(8,128)(2,1)S(1)}, bf16[1024,128]{1,0:T(8,128)(2,1)S(1)}, u32[]{:S(2)}, u32[]{:S(2)}) collective-permute-start(bf16[1024,128]{1,0:T(8,128)(2,1)S(1)} %bitcast.4), channel_id=1, source_target_pairs={{0,8},{8,0},{1,9},{9,1},{2,10},{10,2},{3,11},{11,3},{4,12},{12,4},... | collective-permute-start | bytes 786440 | tf_op jit(solution)/shard_map/ppermute | solution.py:260
  13.9 1.9 %collective-permute-start.1 = (bf16[4,256,128]{2,1,0:T(8,128)(2,1)S(1)}, bf16[4,256,128]{2,1,0:T(8,128)(2,1)S(1)}, u32[]{:S(2)}, u32[]{:S(2)}) collective-permute-start(bf16[4,256,128]{2,1,0:T(8,128)(2,1)S(1)} %all-to-all-done.refs_2_), channel_id=1, source_target_pairs={{0,64},{64,128},{128,192},{192,256},{256,320},{320,384},{384,448},... | collective-permute-start | bytes 786440 | tf_op jit(solution)/shard_map/ppermute | solution.py:272
  15.9 4.6 %collective-permute-start.3 = (bf16[4,256,128]{2,1,0:T(8,128)(2,1)S(1)}, bf16[4,256,128]{2,1,0:T(8,128)(2,1)S(1)}, u32[]{:S(2)}, u32[]{:S(2)}) collective-permute-start(bf16[4,256,128]{2,1,0:T(8,128)(2,1)S(1)} %all-to-all-done.refs_2_), channel_id=1, source_target_pairs={{0,448},{64,0},{128,64},{192,128},{256,192},{320,256},{384,320},{4... | collective-permute-start | bytes 786440 | tf_op jit(solution)/shard_map/ppermute | solution.py:273
  20.4 0.3 shard_map.46.refs_1_
  20.7 2.4 %shard_map.47 = (f32[1,2048]{1,0:T(1,128)S(1)}, f32[1,2048]{1,0:T(1,128)S(1)}, f32[128,2048]{1,0:T(8,128)S(1)}) custom-call(s32[16]{0:T(128)S(1)} %copy-done.1, bf16[256,2048]{1,0:T(8,128)(2,1)S(1)} %shard_map.46.refs_1_, bf16[4,256,128]{2,1,0:T(8,128)(2,1)S(1)} %all-to-all-done.refs_2_), custom_call_target="tpu_custom_call" | custom-call | flops 536870912 | bytes 786432 | tf_op jit(solution)/shard_map/pallas_call | solution.py:216
  23.2 1.9 %collective-permute-start.2 = (bf16[4,256,128]{2,1,0:T(8,128)(2,1)S(1)}, bf16[4,256,128]{2,1,0:T(8,128)(2,1)S(1)}, u32[]{:S(2)}, u32[]{:S(2)}) collective-permute-start(bf16[4,256,128]{2,1,0:T(8,128)(2,1)S(1)} %collective-permute-done.1.refs_2_), channel_id=1, source_target_pairs={{0,64},{64,128},{128,192},{192,256},{256,320},{320,384},{384,448},... | collective-permute-start | bytes 786440 | tf_op jit(solution)/shard_map/ppermute | solution.py:272
  25.1 4.6 %collective-permute-start.6 = (bf16[4,256,128]{2,1,0:T(8,128)(2,1)S(1)}, bf16[4,256,128]{2,1,0:T(8,128)(2,1)S(1)}, u32[]{:S(2)}, u32[]{:S(2)}) collective-permute-start(bf16[4,256,128]{2,1,0:T(8,128)(2,1)S(1)} %collective-permute-done.3.refs_3_), channel_id=1, source_target_pairs={{0,448},{64,0},{128,64},{192,128},{256,192},{320,256},{384,320},{4... | collective-permute-start | bytes 786440 | tf_op jit(solution)/shard_map/ppermute | solution.py:273
  29.7 0.8 %shard_map.48 = (f32[1,2048]{1,0:T(1,128)S(1)}, f32[1,2048]{1,0:T(1,128)S(1)}, f32[128,2048]{1,0:T(8,128)S(1)}) custom-call(s32[16]{0:T(128)S(1)} %copy-done.1, bf16[256,2048]{1,0:T(8,128)(2,1)S(1)} %shard_map.46.refs_1_, bf16[4,256,128]{2,1,0:T(8,128)(2,1)S(1)} %collective-permute-done.1.refs_2_, bf16[4,256,128]{2,1,0:T(8,128)(2,1)S(1)} %collective-permute-done.3.refs_3_, ...), custom_call_target="tpu_custom_call" | custom-call | flops 1073741824 | bytes 1048576 | tf_op jit(solution)/shard_map/pallas_call | solution.py:216
  30.5 1.0 %collective-permute-done.2.refs_2_ = bf16[4,256,128]{2,1,0:T(8,128)(2,1)S(1)} collective-permute-done((bf16[4,256,128]{2,1,0:T(8,128)(2,1)S(1)}, bf16[4,256,128]{2,1,0:T(8,128)(2,1)S(1)}, u32[]{:S(2)}, u32[]{:S(2)}) %collective-permute-start.2) | collective-permute-done | bytes 262176 | tf_op jit(solution)/shard_map/ppermute | solution.py:272
  31.5 1.9 %collective-permute-start.4 = (bf16[4,256,128]{2,1,0:T(8,128)(2,1)S(1)}, bf16[4,256,128]{2,1,0:T(8,128)(2,1)S(1)}, u32[]{:S(2)}, u32[]{:S(2)}) collective-permute-start(bf16[4,256,128]{2,1,0:T(8,128)(2,1)S(1)} %collective-permute-done.2.refs_2_), channel_id=1, source_target_pairs={{0,64},{64,128},{128,192},{192,256},{256,320},{320,384},{384,448},... | collective-permute-start | bytes 786440 | tf_op jit(solution)/shard_map/ppermute | solution.py:272
  33.4 4.6 %collective-permute-start.7 = (bf16[4,256,128]{2,1,0:T(8,128)(2,1)S(1)}, bf16[4,256,128]{2,1,0:T(8,128)(2,1)S(1)}, u32[]{:S(2)}, u32[]{:S(2)}) collective-permute-start(bf16[4,256,128]{2,1,0:T(8,128)(2,1)S(1)} %collective-permute-done.6.refs_3_), channel_id=1, source_target_pairs={{0,448},{64,0},{128,64},{192,128},{256,192},{320,256},{384,320},{4... | collective-permute-start | bytes 786440 | tf_op jit(solution)/shard_map/ppermute | solution.py:273
  38.0 2.0 %collective-permute-done.4.refs_2_ = bf16[4,256,128]{2,1,0:T(8,128)(2,1)S(1)} collective-permute-done((bf16[4,256,128]{2,1,0:T(8,128)(2,1)S(1)}, bf16[4,256,128]{2,1,0:T(8,128)(2,1)S(1)}, u32[]{:S(2)}, u32[]{:S(2)}) %collective-permute-start.4) | collective-permute-done | bytes 262176 | tf_op jit(solution)/shard_map/ppermute | solution.py:272
  40.0 1.9 %collective-permute-start.5 = (bf16[4,256,128]{2,1,0:T(8,128)(2,1)S(1)}, bf16[4,256,128]{2,1,0:T(8,128)(2,1)S(1)}, u32[]{:S(2)}, u32[]{:S(2)}) collective-permute-start(bf16[4,256,128]{2,1,0:T(8,128)(2,1)S(1)} %collective-permute-done.4.refs_2_), channel_id=1, source_target_pairs={{0,64},{64,128},{128,192},{192,256},{256,320},{320,384},{384,448},... | collective-permute-start | bytes 786440 | tf_op jit(solution)/shard_map/ppermute | solution.py:277
  41.9 1.0 %shard_map.49 = (f32[1,2048]{1,0:T(1,128)S(1)}, f32[1,2048]{1,0:T(1,128)S(1)}, f32[128,2048]{1,0:T(8,128)S(1)}) custom-call(s32[16]{0:T(128)S(1)} %copy-done.1, bf16[256,2048]{1,0:T(8,128)(2,1)S(1)} %shard_map.46.refs_1_, bf16[4,256,128]{2,1,0:T(8,128)(2,1)S(1)} %collective-permute-done.2.refs_2_, bf16[4,256,128]{2,1,0:T(8,128)(2,1)S(1)} %collective-permute-done.6.refs_3_, ...), custom_call_target="tpu_custom_call" | custom-call | flops 1073741824 | bytes 1048576 | tf_op jit(solution)/shard_map/pallas_call | solution.py:216
  42.9 1.0 %shard_map.50 = (f32[1,2048]{1,0:T(1,128)S(1)}, f32[1,2048]{1,0:T(1,128)S(1)}, f32[128,2048]{1,0:T(8,128)S(1)}) custom-call(s32[16]{0:T(128)S(1)} %copy-done.1, bf16[256,2048]{1,0:T(8,128)(2,1)S(1)} %shard_map.46.refs_1_, bf16[4,256,128]{2,1,0:T(8,128)(2,1)S(1)} %collective-permute-done.4.refs_2_, bf16[4,256,128]{2,1,0:T(8,128)(2,1)S(1)} %collective-permute-done.7.refs_3_, ...), custom_call_target="tpu_custom_call" | custom-call | flops 1073741824 | bytes 1048576 | tf_op jit(solution)/shard_map/pallas_call | solution.py:216
  44.0 5.6 %collective-permute-done.5.refs_2_ = bf16[4,256,128]{2,1,0:T(8,128)(2,1)S(1)} collective-permute-done((bf16[4,256,128]{2,1,0:T(8,128)(2,1)S(1)}, bf16[4,256,128]{2,1,0:T(8,128)(2,1)S(1)}, u32[]{:S(2)}, u32[]{:S(2)}) %collective-permute-start.5) | collective-permute-done | bytes 262176 | tf_op jit(solution)/shard_map/ppermute | solution.py:277
  49.6 0.8 %shard_map.51 = bf16[144,1024]{1,0:T(8,128)(2,1)S(1)} custom-call(s32[16]{0:T(128)S(1)} %copy-done.1, bf16[256,2048]{1,0:T(8,128)(2,1)S(1)} %shard_map.46.refs_1_, bf16[4,256,128]{2,1,0:T(8,128)(2,1)S(1)} %collective-permute-done.5.refs_2_, f32[1,2048]{1,0:T(1,128)S(1)} %get-tuple-element.52.refs_3_, f32[1,2048]{1,0:T(1,128)S(1)} %get-tuple-element.53.refs_4_, ...), custom_call_target="tpu_custom_call" | custom-call | flops 268435456 | bytes 524288 | tf_op jit(solution)/shard_map/pallas_call | solution.py:216
  50.3 10.5 %collective-permute-start.8 = (bf16[144,1024]{1,0:T(8,128)(2,1)S(1)}, bf16[144,1024]{1,0:T(8,128)(2,1)S(1)}, u32[]{:S(2)}, u32[]{:S(2)}) collective-permute-start(bf16[144,1024]{1,0:T(8,128)(2,1)S(1)} %shard_map.51), channel_id=1, source_target_pairs={{0,8},{8,0},{1,9},{9,1},{2,10},{10,2},{3,11},{11,3},{4,12},{12,4},... | collective-permute-start | bytes 884744 | tf_op jit(solution)/shard_map/ppermute | solution.py:284
  60.8 0.7 %shard_map.52 = (f32[1,1024]{1,0:T(1,128)S(1)}, f32[1,1024]{1,0:T(1,128)S(1)}, f32[128,1024]{1,0:T(8,128)S(1)}) custom-call(s32[16]{0:T(128)S(1)} %copy-done.1, bf16[256,2048]{1,0:T(8,128)(2,1)S(1)} %shard_map.46.refs_1_, bf16[4,256,128]{2,1,0:T(8,128)(2,1)S(1)} %collective-permute-done.5.refs_2_, f32[1,2048]{1,0:T(1,128)S(1)} %get-tuple-element.52.refs_3_, ...), custom_call_target="tpu_custom_call" | custom-call | flops 268435456 | bytes 524288 | tf_op jit(solution)/shard_map/pallas_call | solution.py:216
  61.5 0.5 collective-permute-done.8.p_ref
  62.0 0.9 %shard_map.53 = bf16[1024,128]{1,0:T(8,128)(2,1)} custom-call(f32[1,1024]{1,0:T(1,128)S(1)} %get-tuple-element.55.m_ref, f32[1,1024]{1,0:T(1,128)S(1)} %get-tuple-element.56.l_ref, f32[128,1024]{1,0:T(8,128)S(1)} %get-tuple-element.57.a_ref, bf16[144,1024]{1,0:T(8,128)(2,1)S(1)} %collective-permute-done.8.p_ref), custom_call_target="tpu_custom_call" | custom-call | tf_op jit(solution)/shard_map/pallas_call | solution.py:246
  (13 shorter events, 0.0 us)
Async XLA Ops:
  0.0 0.8 %copy-start.2 = (bf16[128,1,128]{2,0,1:T(8,128)(2,1)S(1)}, bf16[128,1,128]{2,0,1:T(8,128)(2,1)}, u32[]{:S(2)}) copy-start(bf16[128,1,128]{2,0,1:T(8,128)(2,1)} %param.6) | copy-start | bytes 98308
  1.5 5.0 %copy-start = (bf16[128,8,128]{2,1,0:T(8,128)(2,1)S(1)}, bf16[128,8,128]{2,1,0:T(8,128)(2,1)}, u32[]{:S(2)}) copy-start(bf16[128,8,128]{2,1,0:T(8,128)(2,1)} %param.4) | copy-start | bytes 786436
  1.5 12.4 %all-to-all-start = ((bf16[4,256,128]{2,1,0:T(8,128)(2,1)}), bf16[4,256,128]{2,1,0:T(8,128)(2,1)S(1)}, u32[]{:S(2)}, u32[]{:S(2)}) async-start(bf16[4,256,128]{2,1,0:T(8,128)(2,1)} %pad_maximum_fusion), calls=%async_computation | async-start | bytes 524288 | tf_op jit(solution)/shard_map/all_to_all | solution.py:265
  6.5 14.2 %copy-start.1 = (s32[16]{0:T(128)S(1)}, s32[16]{0:T(128)}, u32[]{:S(2)}) copy-start(s32[16]{0:T(128)} %refs_0_.11) | copy-start | bytes 196
  6.5 13.9 %collective-permute-start = (bf16[1024,128]{1,0:T(8,128)(2,1)S(1)}, bf16[1024,128]{1,0:T(8,128)(2,1)S(1)}, u32[]{:S(2)}, u32[]{:S(2)}) collective-permute-start(bf16[1024,128]{1,0:T(8,128)(2,1)S(1)} %bitcast.4), channel_id=1, source_target_pairs={{0,8},{8,0},{1,9},{9,1},{2,10},{10,2},{3,11},{11,3},{4,12},{12,4},... | collective-permute-start | bytes 786440 | tf_op jit(solution)/shard_map/ppermute | solution.py:260
  13.9 9.2 %collective-permute-start.1 = (bf16[4,256,128]{2,1,0:T(8,128)(2,1)S(1)}, bf16[4,256,128]{2,1,0:T(8,128)(2,1)S(1)}, u32[]{:S(2)}, u32[]{:S(2)}) collective-permute-start(bf16[4,256,128]{2,1,0:T(8,128)(2,1)S(1)} %all-to-all-done.refs_2_), channel_id=1, source_target_pairs={{0,64},{64,128},{128,192},{192,256},{256,320},{320,384},{384,448},... | collective-permute-start | bytes 786440 | tf_op jit(solution)/shard_map/ppermute | solution.py:272
  15.9 9.2 %collective-permute-start.3 = (bf16[4,256,128]{2,1,0:T(8,128)(2,1)S(1)}, bf16[4,256,128]{2,1,0:T(8,128)(2,1)S(1)}, u32[]{:S(2)}, u32[]{:S(2)}) collective-permute-start(bf16[4,256,128]{2,1,0:T(8,128)(2,1)S(1)} %all-to-all-done.refs_2_), channel_id=1, source_target_pairs={{0,448},{64,0},{128,64},{192,128},{256,192},{320,256},{384,320},{4... | collective-permute-start | bytes 786440 | tf_op jit(solution)/shard_map/ppermute | solution.py:273
  23.2 8.3 %collective-permute-start.2 = (bf16[4,256,128]{2,1,0:T(8,128)(2,1)S(1)}, bf16[4,256,128]{2,1,0:T(8,128)(2,1)S(1)}, u32[]{:S(2)}, u32[]{:S(2)}) collective-permute-start(bf16[4,256,128]{2,1,0:T(8,128)(2,1)S(1)} %collective-permute-done.1.refs_2_), channel_id=1, source_target_pairs={{0,64},{64,128},{128,192},{192,256},{256,320},{320,384},{384,448},... | collective-permute-start | bytes 786440 | tf_op jit(solution)/shard_map/ppermute | solution.py:272
  25.1 8.3 %collective-permute-start.6 = (bf16[4,256,128]{2,1,0:T(8,128)(2,1)S(1)}, bf16[4,256,128]{2,1,0:T(8,128)(2,1)S(1)}, u32[]{:S(2)}, u32[]{:S(2)}) collective-permute-start(bf16[4,256,128]{2,1,0:T(8,128)(2,1)S(1)} %collective-permute-done.3.refs_3_), channel_id=1, source_target_pairs={{0,448},{64,0},{128,64},{192,128},{256,192},{320,256},{384,320},{4... | collective-permute-start | bytes 786440 | tf_op jit(solution)/shard_map/ppermute | solution.py:273
  31.5 8.5 %collective-permute-start.4 = (bf16[4,256,128]{2,1,0:T(8,128)(2,1)S(1)}, bf16[4,256,128]{2,1,0:T(8,128)(2,1)S(1)}, u32[]{:S(2)}, u32[]{:S(2)}) collective-permute-start(bf16[4,256,128]{2,1,0:T(8,128)(2,1)S(1)} %collective-permute-done.2.refs_2_), channel_id=1, source_target_pairs={{0,64},{64,128},{128,192},{192,256},{256,320},{320,384},{384,448},... | collective-permute-start | bytes 786440 | tf_op jit(solution)/shard_map/ppermute | solution.py:272
  33.4 9.5 %collective-permute-start.7 = (bf16[4,256,128]{2,1,0:T(8,128)(2,1)S(1)}, bf16[4,256,128]{2,1,0:T(8,128)(2,1)S(1)}, u32[]{:S(2)}, u32[]{:S(2)}) collective-permute-start(bf16[4,256,128]{2,1,0:T(8,128)(2,1)S(1)} %collective-permute-done.6.refs_3_), channel_id=1, source_target_pairs={{0,448},{64,0},{128,64},{192,128},{256,192},{320,256},{384,320},{4... | collective-permute-start | bytes 786440 | tf_op jit(solution)/shard_map/ppermute | solution.py:273
  40.0 9.6 %collective-permute-start.5 = (bf16[4,256,128]{2,1,0:T(8,128)(2,1)S(1)}, bf16[4,256,128]{2,1,0:T(8,128)(2,1)S(1)}, u32[]{:S(2)}, u32[]{:S(2)}) collective-permute-start(bf16[4,256,128]{2,1,0:T(8,128)(2,1)S(1)} %collective-permute-done.4.refs_2_), channel_id=1, source_target_pairs={{0,64},{64,128},{128,192},{192,256},{256,320},{320,384},{384,448},... | collective-permute-start | bytes 786440 | tf_op jit(solution)/shard_map/ppermute | solution.py:277
  50.3 11.7 %collective-permute-start.8 = (bf16[144,1024]{1,0:T(8,128)(2,1)S(1)}, bf16[144,1024]{1,0:T(8,128)(2,1)S(1)}, u32[]{:S(2)}, u32[]{:S(2)}) collective-permute-start(bf16[144,1024]{1,0:T(8,128)(2,1)S(1)} %shard_map.51), channel_id=1, source_target_pairs={{0,8},{8,0},{1,9},{9,1},{2,10},{10,2},{3,11},{11,3},{4,12},{12,4},... | collective-permute-start | bytes 884744 | tf_op jit(solution)/shard_map/ppermute | solution.py:284

commit v6 on v5

--- a/solution.py
+++ b/solution.py
@@ -230,11 +230,8 @@
 
 def combine_kernel(m_ref, l_ref, a_ref, p_ref, out_ref):
     depth = a_ref.shape[0]
-    level = (
-        p_ref[depth : depth + 1].astype(jnp.float32)
-        + p_ref[depth + 1 : depth + 2].astype(jnp.float32)
-        + p_ref[depth + 2 : depth + 3].astype(jnp.float32)
-    )
+    tail = p_ref[depth : depth + 16].astype(jnp.float32)
+    level = tail[0:1] + tail[1:2] + tail[2:3]
     top = jnp.maximum(m_ref[...], level)
     here, there = jnp.exp2(m_ref[...] - top), jnp.exp2(level - top)
     whole = 1.0 / (l_ref[...] * here + there)

time: 63.7 us -> 64.2 us (level)
  Pallas kernels: 7.84 us -> 11.8 us
  waiting for transfers between devices: 9.14 us -> 6.01 us
    pallas_call x6, Pallas kernels: 6.67 us -> 10.6 us  [attend(): pl.pallas_call(body, out_shape=out_shape, in_specs=[SM] + [VM] * (len(arg...]
    ppermute x1, waiting for transfers between devices: 5.64 us -> 4.19 us  [local(): farthest = lax.ppermute(rising, 'blk', up)]
    ppermute x3, waiting for transfers between devices: 3 us -> 1.81 us  [local(): rising = lax.ppermute(rising, 'blk', up)]
  transfers between devices with their start and end apart: 10 -> 10, of which waited for: 4 -> 2; matrix products, arithmetic and copies ran while one was open for 0% -> 0% of each run, Pallas kernels for 10% -> 15%
where the time goes in v6:
time: 64.2 us; the launch traced here: 63.6 us
  starting transfers between devices  44 us (69%)
  Pallas kernels  11.8 us (18%)
  waiting for transfers between devices  6.01 us (9%)
  local copies, waits for them, and re-layouts  0.81 us (1%)
  other arithmetic  0.72 us (1%)
    ppermute x3, starting transfers between devices, local(): falling = lax.ppermute(falling, 'blk', back)  13.7 us
    pallas_call x6, Pallas kernels, attend(): pl.pallas_call(body, out_shape=out_shape, in_specs=[SM] + [VM] * (len(arg...  10.6 us
    ppermute x1, starting transfers between devices, local(): theirs = lax.ppermute(packet, 'core', swap)  10.3 us
    ppermute x1, starting transfers between devices, local(): other = lax.ppermute(own, 'core', swap)  7.38 us
    ppermute x3, starting transfers between devices, local(): rising = lax.ppermute(rising, 'blk', up)  5.76 us
    all_to_all x1, starting transfers between devices, local(): row = lax.all_to_all(spread, 'x', 0, 0, tiled=True)  4.97 us
    ppermute x1, waiting for transfers between devices, local(): farthest = lax.ppermute(rising, 'blk', up)  4.19 us
    ppermute x1, starting transfers between devices, local(): farthest = lax.ppermute(rising, 'blk', up)  1.91 us
  transfers between devices with their start and end apart: 10, of which 2 were waited for; matrix products, arithmetic and copies ran while one was open for 0% of the time, Pallas kernels for 15%

profile of v6, /device:TPU:1, one launch (start us, length us, event | category | flops | bytes accessed | tf_op | source)
XLA Modules:
  0.0 63.6 jit_solution(1868715731024907803)
XLA Ops:
  0.0 0.8 %broadcast_in_dim.15 = bf16[4,128,128]{2,1,0:T(8,128)(2,1)S(1)} broadcast(bf16[128,128]{1,0:T(8,128)(2,1)} %bitcast.6), dimensions={1,2} | broadcast | bytes 163840 | tf_op jit(solution)/shard_map/broadcast_in_dim | solution.py:259
  0.8 0.7 %pad_maximum_fusion = bf16[4,256,128]{2,1,0:T(8,128)(2,1)} fusion(bf16[4,128,128]{2,1,0:T(8,128)(2,1)S(1)} %broadcast_in_dim.17, bf16[4,128,128]{2,1,0:T(8,128)(2,1)S(1)} %broadcast_in_dim.15), kind=kLoop, calls=%fused_computation | loop fusion | flops 524288 | bytes 524288 | tf_op jit(solution)/shard_map/concatenate | solution.py:261
  1.5 5.0 %all-to-all-start = ((bf16[4,256,128]{2,1,0:T(8,128)(2,1)}), bf16[4,256,128]{2,1,0:T(8,128)(2,1)S(1)}, u32[]{:S(2)}, u32[]{:S(2)}) async-start(bf16[4,256,128]{2,1,0:T(8,128)(2,1)} %pad_maximum_fusion), calls=%async_computation | async-start | bytes 524288 | tf_op jit(solution)/shard_map/all_to_all | solution.py:262
  6.5 7.4 %collective-permute-start = (bf16[1024,128]{1,0:T(8,128)(2,1)S(1)}, bf16[1024,128]{1,0:T(8,128)(2,1)S(1)}, u32[]{:S(2)}, u32[]{:S(2)}) collective-permute-start(bf16[1024,128]{1,0:T(8,128)(2,1)S(1)} %bitcast.4), channel_id=1, source_target_pairs={{0,8},{8,0},{1,9},{9,1},{2,10},{10,2},{3,11},{11,3},{4,12},{12,4},... | collective-permute-start | bytes 786440 | tf_op jit(solution)/shard_map/ppermute | solution.py:257
  13.9 0.0 all-to-all-done.refs_2_
  13.9 1.9 %collective-permute-start.1 = (bf16[4,256,128]{2,1,0:T(8,128)(2,1)S(1)}, bf16[4,256,128]{2,1,0:T(8,128)(2,1)S(1)}, u32[]{:S(2)}, u32[]{:S(2)}) collective-permute-start(bf16[4,256,128]{2,1,0:T(8,128)(2,1)S(1)} %all-to-all-done.refs_2_), channel_id=1, source_target_pairs={{0,64},{64,128},{128,192},{192,256},{256,320},{320,384},{384,448},... | collective-permute-start | bytes 786440 | tf_op jit(solution)/shard_map/ppermute | solution.py:269
  15.9 4.6 %collective-permute-start.3 = (bf16[4,256,128]{2,1,0:T(8,128)(2,1)S(1)}, bf16[4,256,128]{2,1,0:T(8,128)(2,1)S(1)}, u32[]{:S(2)}, u32[]{:S(2)}) collective-permute-start(bf16[4,256,128]{2,1,0:T(8,128)(2,1)S(1)} %all-to-all-done.refs_2_), channel_id=1, source_target_pairs={{0,448},{64,0},{128,64},{192,128},{256,192},{320,256},{384,320},{4... | collective-permute-start | bytes 786440 | tf_op jit(solution)/shard_map/ppermute | solution.py:270
  20.4 0.0 collective-permute-done.other_ref
  20.4 0.3 shard_map.46.refs_1_
  20.7 2.4 %shard_map.47 = (f32[1,2048]{1,0:T(1,128)S(1)}, f32[1,2048]{1,0:T(1,128)S(1)}, f32[128,2048]{1,0:T(8,128)S(1)}) custom-call(s32[16]{0:T(128)S(1)} %copy-done.1, bf16[256,2048]{1,0:T(8,128)(2,1)S(1)} %shard_map.46.refs_1_, bf16[4,256,128]{2,1,0:T(8,128)(2,1)S(1)} %all-to-all-done.refs_2_), custom_call_target="tpu_custom_call" | custom-call | flops 536870912 | bytes 786432 | tf_op jit(solution)/shard_map/pallas_call | solution.py:216
  23.2 1.9 %collective-permute-start.2 = (bf16[4,256,128]{2,1,0:T(8,128)(2,1)S(1)}, bf16[4,256,128]{2,1,0:T(8,128)(2,1)S(1)}, u32[]{:S(2)}, u32[]{:S(2)}) collective-permute-start(bf16[4,256,128]{2,1,0:T(8,128)(2,1)S(1)} %collective-permute-done.1.refs_2_), channel_id=1, source_target_pairs={{0,64},{64,128},{128,192},{192,256},{256,320},{320,384},{384,448},... | collective-permute-start | bytes 786440 | tf_op jit(solution)/shard_map/ppermute | solution.py:269
  25.1 4.6 %collective-permute-start.6 = (bf16[4,256,128]{2,1,0:T(8,128)(2,1)S(1)}, bf16[4,256,128]{2,1,0:T(8,128)(2,1)S(1)}, u32[]{:S(2)}, u32[]{:S(2)}) collective-permute-start(bf16[4,256,128]{2,1,0:T(8,128)(2,1)S(1)} %collective-permute-done.3.refs_3_), channel_id=1, source_target_pairs={{0,448},{64,0},{128,64},{192,128},{256,192},{320,256},{384,320},{4... | collective-permute-start | bytes 786440 | tf_op jit(solution)/shard_map/ppermute | solution.py:270
  29.7 2.0 %shard_map.48 = (f32[1,2048]{1,0:T(1,128)S(1)}, f32[1,2048]{1,0:T(1,128)S(1)}, f32[128,2048]{1,0:T(8,128)S(1)}) custom-call(s32[16]{0:T(128)S(1)} %copy-done.1, bf16[256,2048]{1,0:T(8,128)(2,1)S(1)} %shard_map.46.refs_1_, bf16[4,256,128]{2,1,0:T(8,128)(2,1)S(1)} %collective-permute-done.1.refs_2_, bf16[4,256,128]{2,1,0:T(8,128)(2,1)S(1)} %collective-permute-done.3.refs_3_, ...), custom_call_target="tpu_custom_call" | custom-call | flops 1073741824 | bytes 1048576 | tf_op jit(solution)/shard_map/pallas_call | solution.py:216
  31.7 1.9 %collective-permute-start.4 = (bf16[4,256,128]{2,1,0:T(8,128)(2,1)S(1)}, bf16[4,256,128]{2,1,0:T(8,128)(2,1)S(1)}, u32[]{:S(2)}, u32[]{:S(2)}) collective-permute-start(bf16[4,256,128]{2,1,0:T(8,128)(2,1)S(1)} %collective-permute-done.2.refs_2_), channel_id=1, source_target_pairs={{0,64},{64,128},{128,192},{192,256},{256,320},{320,384},{384,448},... | collective-permute-start | bytes 786440 | tf_op jit(solution)/shard_map/ppermute | solution.py:269
  33.7 4.6 %collective-permute-start.7 = (bf16[4,256,128]{2,1,0:T(8,128)(2,1)S(1)}, bf16[4,256,128]{2,1,0:T(8,128)(2,1)S(1)}, u32[]{:S(2)}, u32[]{:S(2)}) collective-permute-start(bf16[4,256,128]{2,1,0:T(8,128)(2,1)S(1)} %collective-permute-done.6.refs_3_), channel_id=1, source_target_pairs={{0,448},{64,0},{128,64},{192,128},{256,192},{320,256},{384,320},{4... | collective-permute-start | bytes 786440 | tf_op jit(solution)/shard_map/ppermute | solution.py:270
  38.3 1.8 %collective-permute-done.4.refs_2_ = bf16[4,256,128]{2,1,0:T(8,128)(2,1)S(1)} collective-permute-done((bf16[4,256,128]{2,1,0:T(8,128)(2,1)S(1)}, bf16[4,256,128]{2,1,0:T(8,128)(2,1)S(1)}, u32[]{:S(2)}, u32[]{:S(2)}) %collective-permute-start.4) | collective-permute-done | bytes 262176 | tf_op jit(solution)/shard_map/ppermute | solution.py:269
  40.1 1.9 %collective-permute-start.5 = (bf16[4,256,128]{2,1,0:T(8,128)(2,1)S(1)}, bf16[4,256,128]{2,1,0:T(8,128)(2,1)S(1)}, u32[]{:S(2)}, u32[]{:S(2)}) collective-permute-start(bf16[4,256,128]{2,1,0:T(8,128)(2,1)S(1)} %collective-permute-done.4.refs_2_), channel_id=1, source_target_pairs={{0,64},{64,128},{128,192},{192,256},{256,320},{320,384},{384,448},... | collective-permute-start | bytes 786440 | tf_op jit(solution)/shard_map/ppermute | solution.py:274
  42.0 2.2 %shard_map.49 = (f32[1,2048]{1,0:T(1,128)S(1)}, f32[1,2048]{1,0:T(1,128)S(1)}, f32[128,2048]{1,0:T(8,128)S(1)}) custom-call(s32[16]{0:T(128)S(1)} %copy-done.1, bf16[256,2048]{1,0:T(8,128)(2,1)S(1)} %shard_map.46.refs_1_, bf16[4,256,128]{2,1,0:T(8,128)(2,1)S(1)} %collective-permute-done.2.refs_2_, bf16[4,256,128]{2,1,0:T(8,128)(2,1)S(1)} %collective-permute-done.6.refs_3_, ...), custom_call_target="tpu_custom_call" | custom-call | flops 1073741824 | bytes 1048576 | tf_op jit(solution)/shard_map/pallas_call | solution.py:216
  44.2 1.0 %shard_map.50 = (f32[1,2048]{1,0:T(1,128)S(1)}, f32[1,2048]{1,0:T(1,128)S(1)}, f32[128,2048]{1,0:T(8,128)S(1)}) custom-call(s32[16]{0:T(128)S(1)} %copy-done.1, bf16[256,2048]{1,0:T(8,128)(2,1)S(1)} %shard_map.46.refs_1_, bf16[4,256,128]{2,1,0:T(8,128)(2,1)S(1)} %collective-permute-done.4.refs_2_, bf16[4,256,128]{2,1,0:T(8,128)(2,1)S(1)} %collective-permute-done.7.refs_3_, ...), custom_call_target="tpu_custom_call" | custom-call | flops 1073741824 | bytes 1048576 | tf_op jit(solution)/shard_map/pallas_call | solution.py:216
  45.3 4.2 %collective-permute-done.5.refs_2_ = bf16[4,256,128]{2,1,0:T(8,128)(2,1)S(1)} collective-permute-done((bf16[4,256,128]{2,1,0:T(8,128)(2,1)S(1)}, bf16[4,256,128]{2,1,0:T(8,128)(2,1)S(1)}, u32[]{:S(2)}, u32[]{:S(2)}) %collective-permute-start.5) | collective-permute-done | bytes 262176 | tf_op jit(solution)/shard_map/ppermute | solution.py:274
  49.5 1.5 %shard_map.51 = bf16[144,1024]{1,0:T(8,128)(2,1)S(1)} custom-call(s32[16]{0:T(128)S(1)} %copy-done.1, bf16[256,2048]{1,0:T(8,128)(2,1)S(1)} %shard_map.46.refs_1_, bf16[4,256,128]{2,1,0:T(8,128)(2,1)S(1)} %collective-permute-done.5.refs_2_, f32[1,2048]{1,0:T(1,128)S(1)} %get-tuple-element.52.refs_3_, f32[1,2048]{1,0:T(1,128)S(1)} %get-tuple-element.53.refs_4_, ...), custom_call_target="tpu_custom_call" | custom-call | flops 268435456 | bytes 524288 | tf_op jit(solution)/shard_map/pallas_call | solution.py:216
  51.0 10.3 %collective-permute-start.8 = (bf16[144,1024]{1,0:T(8,128)(2,1)S(1)}, bf16[144,1024]{1,0:T(8,128)(2,1)S(1)}, u32[]{:S(2)}, u32[]{:S(2)}) collective-permute-start(bf16[144,1024]{1,0:T(8,128)(2,1)S(1)} %shard_map.51), channel_id=1, source_target_pairs={{0,8},{8,0},{1,9},{9,1},{2,10},{10,2},{3,11},{11,3},{4,12},{12,4},... | collective-permute-start | bytes 884744 | tf_op jit(solution)/shard_map/ppermute | solution.py:281
  61.2 1.4 %shard_map.52 = (f32[1,1024]{1,0:T(1,128)S(1)}, f32[1,1024]{1,0:T(1,128)S(1)}, f32[128,1024]{1,0:T(8,128)S(1)}) custom-call(s32[16]{0:T(128)S(1)} %copy-done.1, bf16[256,2048]{1,0:T(8,128)(2,1)S(1)} %shard_map.46.refs_1_, bf16[4,256,128]{2,1,0:T(8,128)(2,1)S(1)} %collective-permute-done.5.refs_2_, f32[1,2048]{1,0:T(1,128)S(1)} %get-tuple-element.52.refs_3_, ...), custom_call_target="tpu_custom_call" | custom-call | flops 268435456 | bytes 524288 | tf_op jit(solution)/shard_map/pallas_call | solution.py:216
  62.7 0.9 %shard_map.53 = bf16[1024,128]{1,0:T(8,128)(2,1)} custom-call(f32[1,1024]{1,0:T(1,128)S(1)} %get-tuple-element.55.m_ref, f32[1,1024]{1,0:T(1,128)S(1)} %get-tuple-element.56.l_ref, f32[128,1024]{1,0:T(8,128)S(1)} %get-tuple-element.57.a_ref, bf16[144,1024]{1,0:T(8,128)(2,1)S(1)} %collective-permute-done.8.p_ref), custom_call_target="tpu_custom_call" | custom-call | tf_op jit(solution)/shard_map/pallas_call | solution.py:243
  (13 shorter events, 0.0 us)
Async XLA Ops:
  0.0 0.8 %copy-start.2 = (bf16[128,1,128]{2,0,1:T(8,128)(2,1)S(1)}, bf16[128,1,128]{2,0,1:T(8,128)(2,1)}, u32[]{:S(2)}) copy-start(bf16[128,1,128]{2,0,1:T(8,128)(2,1)} %param.6) | copy-start | bytes 98308
  1.5 5.0 %copy-start = (bf16[128,8,128]{2,1,0:T(8,128)(2,1)S(1)}, bf16[128,8,128]{2,1,0:T(8,128)(2,1)}, u32[]{:S(2)}) copy-start(bf16[128,8,128]{2,1,0:T(8,128)(2,1)} %param.4) | copy-start | bytes 786436
  1.5 12.4 %all-to-all-start = ((bf16[4,256,128]{2,1,0:T(8,128)(2,1)}), bf16[4,256,128]{2,1,0:T(8,128)(2,1)S(1)}, u32[]{:S(2)}, u32[]{:S(2)}) async-start(bf16[4,256,128]{2,1,0:T(8,128)(2,1)} %pad_maximum_fusion), calls=%async_computation | async-start | bytes 524288 | tf_op jit(solution)/shard_map/all_to_all | solution.py:262
  6.5 14.2 %copy-start.1 = (s32[16]{0:T(128)S(1)}, s32[16]{0:T(128)}, u32[]{:S(2)}) copy-start(s32[16]{0:T(128)} %refs_0_.11) | copy-start | bytes 196
  6.5 13.9 %collective-permute-start = (bf16[1024,128]{1,0:T(8,128)(2,1)S(1)}, bf16[1024,128]{1,0:T(8,128)(2,1)S(1)}, u32[]{:S(2)}, u32[]{:S(2)}) collective-permute-start(bf16[1024,128]{1,0:T(8,128)(2,1)S(1)} %bitcast.4), channel_id=1, source_target_pairs={{0,8},{8,0},{1,9},{9,1},{2,10},{10,2},{3,11},{11,3},{4,12},{12,4},... | collective-permute-start | bytes 786440 | tf_op jit(solution)/shard_map/ppermute | solution.py:257
  13.9 9.2 %collective-permute-start.1 = (bf16[4,256,128]{2,1,0:T(8,128)(2,1)S(1)}, bf16[4,256,128]{2,1,0:T(8,128)(2,1)S(1)}, u32[]{:S(2)}, u32[]{:S(2)}) collective-permute-start(bf16[4,256,128]{2,1,0:T(8,128)(2,1)S(1)} %all-to-all-done.refs_2_), channel_id=1, source_target_pairs={{0,64},{64,128},{128,192},{192,256},{256,320},{320,384},{384,448},... | collective-permute-start | bytes 786440 | tf_op jit(solution)/shard_map/ppermute | solution.py:269
  15.9 9.2 %collective-permute-start.3 = (bf16[4,256,128]{2,1,0:T(8,128)(2,1)S(1)}, bf16[4,256,128]{2,1,0:T(8,128)(2,1)S(1)}, u32[]{:S(2)}, u32[]{:S(2)}) collective-permute-start(bf16[4,256,128]{2,1,0:T(8,128)(2,1)S(1)} %all-to-all-done.refs_2_), channel_id=1, source_target_pairs={{0,448},{64,0},{128,64},{192,128},{256,192},{320,256},{384,320},{4... | collective-permute-start | bytes 786440 | tf_op jit(solution)/shard_map/ppermute | solution.py:270
  23.2 8.6 %collective-permute-start.2 = (bf16[4,256,128]{2,1,0:T(8,128)(2,1)S(1)}, bf16[4,256,128]{2,1,0:T(8,128)(2,1)S(1)}, u32[]{:S(2)}, u32[]{:S(2)}) collective-permute-start(bf16[4,256,128]{2,1,0:T(8,128)(2,1)S(1)} %collective-permute-done.1.refs_2_), channel_id=1, source_target_pairs={{0,64},{64,128},{128,192},{192,256},{256,320},{320,384},{384,448},... | collective-permute-start | bytes 786440 | tf_op jit(solution)/shard_map/ppermute | solution.py:269
  25.1 8.6 %collective-permute-start.6 = (bf16[4,256,128]{2,1,0:T(8,128)(2,1)S(1)}, bf16[4,256,128]{2,1,0:T(8,128)(2,1)S(1)}, u32[]{:S(2)}, u32[]{:S(2)}) collective-permute-start(bf16[4,256,128]{2,1,0:T(8,128)(2,1)S(1)} %collective-permute-done.3.refs_3_), channel_id=1, source_target_pairs={{0,448},{64,0},{128,64},{192,128},{256,192},{320,256},{384,320},{4... | collective-permute-start | bytes 786440 | tf_op jit(solution)/shard_map/ppermute | solution.py:270
  31.7 8.3 %collective-permute-start.4 = (bf16[4,256,128]{2,1,0:T(8,128)(2,1)S(1)}, bf16[4,256,128]{2,1,0:T(8,128)(2,1)S(1)}, u32[]{:S(2)}, u32[]{:S(2)}) collective-permute-start(bf16[4,256,128]{2,1,0:T(8,128)(2,1)S(1)} %collective-permute-done.2.refs_2_), channel_id=1, source_target_pairs={{0,64},{64,128},{128,192},{192,256},{256,320},{320,384},{384,448},... | collective-permute-start | bytes 786440 | tf_op jit(solution)/shard_map/ppermute | solution.py:269
  33.7 10.5 %collective-permute-start.7 = (bf16[4,256,128]{2,1,0:T(8,128)(2,1)S(1)}, bf16[4,256,128]{2,1,0:T(8,128)(2,1)S(1)}, u32[]{:S(2)}, u32[]{:S(2)}) collective-permute-start(bf16[4,256,128]{2,1,0:T(8,128)(2,1)S(1)} %collective-permute-done.6.refs_3_), channel_id=1, source_target_pairs={{0,448},{64,0},{128,64},{192,128},{256,192},{320,256},{384,320},{4... | collective-permute-start | bytes 786440 | tf_op jit(solution)/shard_map/ppermute | solution.py:270
  40.1 9.4 %collective-permute-start.5 = (bf16[4,256,128]{2,1,0:T(8,128)(2,1)S(1)}, bf16[4,256,128]{2,1,0:T(8,128)(2,1)S(1)}, u32[]{:S(2)}, u32[]{:S(2)}) collective-permute-start(bf16[4,256,128]{2,1,0:T(8,128)(2,1)S(1)} %collective-permute-done.4.refs_2_), channel_id=1, source_target_pairs={{0,64},{64,128},{128,192},{192,256},{256,320},{320,384},{384,448},... | collective-permute-start | bytes 786440 | tf_op jit(solution)/shard_map/ppermute | solution.py:274
  51.0 11.7 %collective-permute-start.8 = (bf16[144,1024]{1,0:T(8,128)(2,1)S(1)}, bf16[144,1024]{1,0:T(8,128)(2,1)S(1)}, u32[]{:S(2)}, u32[]{:S(2)}) collective-permute-start(bf16[144,1024]{1,0:T(8,128)(2,1)S(1)} %shard_map.51), channel_id=1, source_target_pairs={{0,8},{8,0},{1,9},{9,1},{2,10},{10,2},{3,11},{11,3},{4,12},{12,4},... | collective-permute-start | bytes 884744 | tf_op jit(solution)/shard_map/ppermute | solution.py:281
